TPU v7x, 256 devices: a whole 4x4x8 slice. The times are simulated.
256 devices in a mesh: dp: 64 (over z, y, x_hi), tensor: 4 (over x_lo, core).
Axes of the slice: x: 4 (x_hi: 2, x_lo: 2; x = x_hi * 2 + x_lo), y: 4, z: 8, core: 2. Of those that a mesh axis runs over, the one named last changes fastest.
Arguments:
- final_input: bfloat16 [32768, 4096], P('dp'), may hold values from -20 to 20
- norm_gain: bfloat16 [4096], replicated, may hold values from 0.5 to 2
- value_weight: bfloat16 [4096, 1024], P(None, 'tensor'), may hold values from -0.09375 to 0.09375
- out_weight: bfloat16 [4096, 4096], P('tensor'), may hold values from -0.1875 to 0.1875
- cluster: int32 [32768, 1], P('dp'), may hold values from 0 to 255; in each aligned block of 512 rows (0 to 511, 512 to 1023, ...) at most 4 rows name the same one
- priority: int32 [32768], P('dp'), may hold values from 0 to 32767, each once
Outputs:
- best_match: float32 [32768], P('dp')
Inputs may be any that keep to these rules, and one draw needn't show every extreme that they name: Among the rows of one device (aligned blocks of 512 documents), no cluster holds more than 4 documents, and some cluster holds exactly 4. `priority`: every rank appears exactly once.
All inputs are finite; a program needn't handle non-finite values.
Results may differ from a plain program's by a relative error of at most 0.0012.
Values may be sent and summed in bfloat16 or wider, within the bound.
No kernel may reach another device: no remote copies, remote signals or barrier semaphores. Data moves between devices by JAX's collectives and lax.ppermute only.
A program may use at most 128 MiB of HBM per device.

v0:
```python
import jax
import jax.numpy as jnp
from jax import lax
from jax.sharding import PartitionSpec as P

HEADS = 32
KV_HEADS = 8
HEAD_DIM = 128
CLU_DEV = 4


def tile_products(members):
    number_items = members.shape[1]
    slot_count = members.shape[0] * members.shape[2]
    products = jnp.einsum(
        "acbf,ecdf->cabed",
        members,
        members,
        precision=lax.Precision.HIGHEST,
        preferred_element_type=jnp.float32,
    )
    return products.reshape(number_items, slot_count, slot_count)


def cluster_best(products, ranking, sentinel):
    number_items = ranking.shape[1]
    ordered = jnp.transpose(ranking, (1, 0, 2)).reshape(number_items, -1)
    allowed = (ordered[:, None, :] < ordered[:, :, None]) & (ordered[:, None, :] < sentinel)
    highest = jnp.max(jnp.where(allowed, products, -2.0), axis=2)
    highest = jnp.maximum(highest, -1.0)
    return jnp.transpose(
        highest.reshape(number_items, ranking.shape[0], ranking.shape[2]), (1, 0, 2)
    )


def head_terms(values, out_weight, kv_local, group_size):
    model_width = out_weight.shape[1]
    folded = jnp.sum(
        out_weight.reshape(kv_local, group_size, HEAD_DIM, model_width).astype(jnp.float32), axis=1
    )
    folded = folded.reshape(kv_local * HEAD_DIM, model_width)
    upper_part = folded.astype(jnp.bfloat16)
    lower_part = (folded - upper_part.astype(jnp.float32)).astype(jnp.bfloat16)
    upper_term = jnp.dot(values, upper_part, preferred_element_type=jnp.float32)
    return upper_term + jnp.dot(values, lower_part, preferred_element_type=jnp.float32)


def shards(final_input, norm_gain, value_weight, out_weight, cluster, priority):
    doc_rows = final_input.shape[0]
    model_width = final_input.shape[1]
    splits = lax.axis_size("tensor")
    owners = lax.axis_size("dp")
    feature_part = model_width // splits
    bucket_size = max(2, 2 * doc_rows // (CLU_DEV * owners))
    sentinel = owners * doc_rows
    inputs_f32 = final_input.astype(jnp.float32)
    scaling = lax.rsqrt(jnp.mean(inputs_f32 * inputs_f32, axis=1, keepdims=True) + 1e-05)
    normed = (inputs_f32 * scaling * norm_gain.astype(jnp.float32)).astype(jnp.bfloat16)
    values = jnp.dot(normed, value_weight, preferred_element_type=jnp.float32).astype(jnp.bfloat16)
    kv_local = value_weight.shape[1] // HEAD_DIM
    group_size = HEADS // KV_HEADS
    partial_out = (
        head_terms(values, out_weight, kv_local, group_size)
        .astype(jnp.bfloat16)
        .astype(jnp.float32)
    )
    feature_start = lax.axis_index("tensor") * feature_part
    summed = lax.psum(partial_out.astype(jnp.bfloat16), "tensor").astype(jnp.float32)
    hidden_full = inputs_f32 + summed
    squares = jnp.sum(hidden_full * hidden_full, axis=1)
    hidden = lax.dynamic_slice_in_dim(hidden_full, feature_start, feature_part, 1)
    embedded = hidden * lax.rsqrt(squares + 1e-06)[:, None]
    cluster_ids = cluster[:, 0]
    positions = jnp.arange(doc_rows, dtype=jnp.int32)
    earlier = (cluster_ids[:, None] == cluster_ids[None, :]) & (
        positions[None, :] < positions[:, None]
    )
    slot_index = jnp.sum(earlier.astype(jnp.int32), axis=1)
    flat_slot = cluster_ids * bucket_size + slot_index
    slot_total = owners * CLU_DEV * bucket_size
    send_rows = jnp.zeros((slot_total, feature_part), jnp.float32).at[flat_slot].set(embedded)
    send_rows = send_rows.reshape(owners, CLU_DEV, bucket_size, feature_part)
    send_ranks = jnp.full((slot_total,), sentinel, jnp.int32).at[flat_slot].set(priority)
    send_ranks = send_ranks.reshape(owners, CLU_DEV, bucket_size)
    members = lax.all_to_all(send_rows, "dp", split_axis=0, concat_axis=0, tiled=True)
    ranking = lax.all_to_all(send_ranks, "dp", split_axis=0, concat_axis=0, tiled=True)
    products = lax.psum(tile_products(members), "tensor")
    highest = cluster_best(products, ranking, sentinel)
    returned = lax.all_to_all(highest, "dp", split_axis=0, concat_axis=0, tiled=True)
    return returned.reshape(-1)[flat_slot]


def solution(mesh):
    in_specs = (P("dp", None), P(), P(None, "tensor"), P("tensor", None), P("dp", None), P("dp"))
    out_specs = P("dp")
    return jax.shard_map(shards, mesh=mesh, in_specs=in_specs, out_specs=out_specs, check_vma=False)
```

profile of v0, /device:TPU:1, one launch (start us, length us, event | category | flops | bytes accessed | tf_op | source)
XLA Modules:
  0.0 387.7 jit_solution(14150619591756824939)
XLA Ops:
  6.5 0.0 copy-start
  6.5 0.0 all-reduce.3.cloned.1.call-start
  6.5 5.5 %convert_reduce_fusion = f32[2,128,4096]{2,1,0:T(8,128)S(1)} fusion(bf16[2,4,128,4096]{3,2,1,0:T(8,128)(2,1)} %bitcast.23), kind=kLoop, calls=%fused_computation.3 | loop fusion | flops 7340032 | bytes 12582912 | tf_op jit(solution)/shard_map/reduce_sum | solution.py:38
  12.1 0.0 copy-start.4
  12.1 0.0 copy-start.2
  12.1 0.6 fusion.8
  12.7 0.1 copy-done.4
  12.8 1.5 copy-done.2
  14.3 0.9 fusion
  15.2 0.0 copy-done
  15.2 1.3 fusion.15
  16.5 1.3 fusion.22
  17.8 3.2 add_convert_fusion
  21.0 0.0 copy-start.3
  21.0 0.0 all-reduce.3.cloned.1.call-update
  21.0 0.0 all-reduce.5.cloned.1.call-start
  21.1 0.6 copy-done.3
  21.7 0.2 convert_reduce_fusion.1
  21.9 100.0 %all-reduce.3.cloned.1.call-done = bf16[512,4096]{1,0:T(8,128)(2,1)} async-done(((bf16[512,4096]{1,0:T(8,128)(2,1)}), bf16[512,4096]{1,0:T(8,128)(2,1)}) %all-reduce.3.cloned.1.call-update) | async-done | bytes 4194320 | tf_op jit(solution)/shard_map/psum | solution.py:68
  121.9 8.0 %multiply_reduce_fusion = (f32[512]{0:T(512)S(1)}, f32[512,4096]{1,0:T(8,128)}) fusion(bf16[512,4096]{1,0:T(8,128)(2,1)} %all-reduce.3.cloned.1.call-done, bf16[512,4096]{1,0:T(8,128)(2,1)} %param.6), kind=kLoop, calls=%fused_computation.10 | loop fusion | flops 10485248 | bytes 16779264 | tf_op jit(solution)/shard_map/reduce_sum | solution.py:70
  129.9 5.7 %scatter_custom_fusion.1 = f32[1024,1024]{1,0:T(8,128)} fusion(s32[512]{0:T(512)S(1)} %bitcast.27, f32[512,4096]{1,0:T(8,128)} %get-tuple-element.8, s32[]{:T(128)} %constant.15.clone.1, s32[]{:T(128)S(6)} %select_n.14, f32[]{:T(128)} %constant.17.clone.1, f32[512]{0:T(512)S(1)} %add_rsqrt_fusion), kind=kCustom, calls=%fused_computation.21 | custom fusion | flops 524288 | bytes 6294532 | tf_op jit(solution)/shard_map/scatter | solution.py:81
  135.6 5.2 %reshape.48 = f32[64,4,4,1024]{3,2,1,0:T(4,128)} reshape(f32[1024,1024]{1,0:T(8,128)} %scatter_custom_fusion.1) | data formatting | bytes 8388608 | tf_op jit(solution)/shard_map/reshape | solution.py:82
  140.8 106.8 %all_to_all.15 = f32[64,4,4,1024]{3,2,1,0:T(4,128)S(1)} all-to-all(f32[64,4,4,1024]{3,2,1,0:T(4,128)} %reshape.48), channel_id=1, replica_groups=mesh['dp'=64,'tensor'=4] {'dp'}, dimensions={0} | all-to-all | bytes 8388608 | tf_op jit(solution)/shard_map/all_to_all | solution.py:85
  247.6 11.3 %fusion.5 = f32[4,64,4,64,4]{3,1,4,2,0:T(8,128)S(1)} fusion(f32[64,4,4,1024,1]{3,2,1,0,4:T(4,128)S(1)} %bitcast.22), kind=kOutput, calls=%fused_computation.13 | convolution fusion | flops 3221225472 | bytes 5242880 | tf_op jit(solution)/shard_map/acbf,ecdf->cabed/dot_general | solution.py:15
  258.9 17.1 %copy.19 = f32[4,64,4,64,4]{4,3,2,1,0:T(8,128)} copy(f32[4,64,4,64,4]{3,1,4,2,0:T(8,128)S(1)} %fusion.5) | data formatting | bytes 2097152 | tf_op jit(solution)/shard_map/acbf,ecdf->cabed/dot_general | solution.py:15
  276.0 0.0 copy-start.1
  276.0 29.3 %reshape.49 = f32[4,256,256]{2,1,0:T(8,128)} reshape(f32[4,64,4,64,4]{4,3,2,1,0:T(8,128)} %copy.19) | data formatting | bytes 2097152 | tf_op jit(solution)/shard_map/reshape | solution.py:22
  305.3 0.0 all-reduce.5.cloned.1.call-update
  305.3 2.6 scatter_custom_fusion
  308.0 0.2 reshape.46
  308.2 19.4 %all_to_all.16 = s32[64,4,4]{2,1,0:T(4,128)S(1)} all-to-all(s32[64,4,4]{2,1,0:T(4,128)S(1)} %reshape.46), channel_id=1, replica_groups=mesh['dp'=64,'tensor'=4] {'dp'}, dimensions={0} | all-to-all | bytes 8192 | tf_op jit(solution)/shard_map/all_to_all | solution.py:86
  327.6 0.1 lt.52
  327.7 23.4 %all-reduce.5.cloned.1.call-done = f32[4,256,256]{2,1,0:T(8,128)} async-done(((f32[4,256,256]{2,1,0:T(8,128)}), f32[4,256,256]{2,1,0:T(8,128)}) %all-reduce.5.cloned.1.call-update) | async-done | bytes 1048592 | tf_op jit(solution)/shard_map/psum | solution.py:87
  351.1 1.6 select_reduce_fusion
  352.8 0.1 max.12
  352.9 0.7 copy.20
  353.6 12.3 %all-to-all-start.2 = ((f32[64,4,4]{2,1,0:T(4,128)}), f32[64,4,4]{2,1,0:T(4,128)S(1)}, u32[]{:S(2)}, u32[]{:S(2)}) async-start(f32[64,4,4]{2,1,0:T(4,128)} %copy.20), calls=%async_computation.2 | async-start | bytes 262144 | tf_op jit(solution)/shard_map/all_to_all | solution.py:89
  366.0 11.3 %all-to-all-done.2 = f32[64,4,4]{2,1,0:T(4,128)S(1)} async-done(((f32[64,4,4]{2,1,0:T(4,128)}), f32[64,4,4]{2,1,0:T(4,128)S(1)}, u32[]{:S(2)}, u32[]{:S(2)}) %all-to-all-start.2) | async-done | bytes 4128 | tf_op jit(solution)/shard_map/all_to_all | solution.py:89
  377.3 0.2 reshape.50
  377.4 3.4 gather_fusion
  380.9 0.0 copy-done.1
  (8 shorter events, 0.1 us)
Async XLA Ops:
  6.5 8.6 %copy-start = (bf16[4096,256]{1,0:T(8,128)(2,1)S(1)}, bf16[4096,256]{1,0:T(8,128)(2,1)}, u32[]{:S(2)}) copy-start(bf16[4096,256]{1,0:T(8,128)(2,1)} %param.8) | copy-start | bytes 6291460
  6.5 115.4 %all-reduce.3.cloned.1.call-start = ((), (), s32[]{:S(2)}) async-start(), calls=%async_computation.3 | async-start | bytes 8388608 | tf_op jit(solution)/shard_map/psum | solution.py:68
  12.1 0.7 copy-start.4
  12.1 2.2 copy-start.2
  21.0 0.7 copy-start.3
  21.0 330.1 %all-reduce.5.cloned.1.call-start = ((), (), s32[]{:S(2)}) async-start(), calls=%async_computation.4 | async-start | bytes 2097152 | tf_op jit(solution)/shard_map/psum | solution.py:87
  276.0 104.8 %copy-start.1 = (bf16[4096,256]{1,0:T(8,128)(2,1)S(1)}, bf16[4096,256]{1,0:T(8,128)(2,1)}, u32[]{:S(2)}) copy-start(bf16[4096,256]{1,0:T(8,128)(2,1)} %param.8) | copy-start | bytes 6291460
  353.6 23.6 %all-to-all-start.2 = ((f32[64,4,4]{2,1,0:T(4,128)}), f32[64,4,4]{2,1,0:T(4,128)S(1)}, u32[]{:S(2)}, u32[]{:S(2)}) async-start(f32[64,4,4]{2,1,0:T(4,128)} %copy.20), calls=%async_computation.2 | async-start | bytes 262144 | tf_op jit(solution)/shard_map/all_to_all | solution.py:89
Sparse Core Ops, SparseCore 0:
  21.1 100.7 all-reduce.2
  305.5 45.6 all-reduce.4
where the time goes:
time: 388 us
  waiting for transfers between devices  135 us (35%)
  blocking collectives  126 us (32%)
  local copies, waits for them, and re-layouts  61.1 us (16%)
  other arithmetic  22.6 us (6%)
  matrix products  17.1 us (4%)
  between operations  13.5 us (3%)
  starting transfers between devices  12.4 us (3%)
    all_to_all x1, blocking collectives, shards(): lax.all_to_all(send_rows, 'dp', split_axis=0, concat_axis=0, tiled=True)  107 us
    psum x1, waiting for transfers between devices, shards(): lax.psum(partial_out.astype(jnp.bfloat16), 'tensor').astype(jnp.float32)  100 us
    reshape x1, local copies, waits for them, and re-layouts, tile_products(): return products.reshape(number_items, slot_count, slot_count)  29.3 us
    psum x1, waiting for transfers between devices, shards(): products = lax.psum(tile_products(members), 'tensor')  23.4 us
    all_to_all x1, blocking collectives, shards(): lax.all_to_all(send_ranks, 'dp', split_axis=0, concat_axis=0, tiled=True)  19.4 us
    dot_general x1, local copies, waits for them, and re-layouts, tile_products(): jnp.einsum('acbf,ecdf->cabed', members, members, precision=lax.Precision....  17.1 us
    all_to_all x1, starting transfers between devices, shards(): lax.all_to_all(highest, 'dp', split_axis=0, concat_axis=0, tiled=True)  12.3 us
    dot_general x1, matrix products, tile_products(): jnp.einsum('acbf,ecdf->cabed', members, members, precision=lax.Precision....  11.3 us
  transfers between devices with their start and end apart: 3, of which 3 were waited for; matrix products, arithmetic and copies ran while one was open for 1% of the time, Pallas kernels for 0%

commit v1 on v0

v1 whole, which is shorter than its diff:
```python
import jax
import jax.numpy as jnp
from jax import lax
from jax.experimental import pallas as pl
from jax.experimental.pallas import tpu as pltpu
from jax.sharding import PartitionSpec as P

HEADS = 32
KV_HEADS = 8
HEAD_DIM = 128
SLOTS = 4
LANES = 128
AXES = ("dp", "tensor")
F32 = jnp.float32
BF16 = jnp.bfloat16
MIB = 2**20
COLUMN_PARTS = 8
ROW_PARTS = 4
RANK_BASE = 128


def iota(shape, dim):
    return lax.broadcasted_iota(jnp.int32, shape, dim)


def chosen(flat_row, clusters, slot):
    rows = flat_row.shape[1]
    wanted = iota((clusters, rows), 0) * SLOTS + slot
    return flat_row == wanted


def blocks(width):
    return width // LANES


def pack_kernel(
    me_ref, cluster_ref, priority_ref, gain_ref, x_hbm, weight_hbm,
    flat_ref, message_hbm,
    x_ref, weight_ref, wide_ref, message_ref, select_ref, square_ref, in_sems, out_sems,
):
    rows, width = x_ref.shape
    clusters = select_ref.shape[1]
    depth = wide_ref.shape[0] // clusters
    me = me_ref[0]
    sentinel = me_ref[1]
    part = width // COLUMN_PARTS
    x_copies = []
    for j in range(COLUMN_PARTS):
        cols = pl.ds(j * part, part)
        copy = pltpu.make_async_copy(x_hbm.at[:, cols], x_ref.at[:, cols], in_sems.at[j])
        copy.start()
        x_copies.append(copy)
    weight_copy = pltpu.make_async_copy(weight_hbm, weight_ref, in_sems.at[COLUMN_PARTS])
    weight_copy.start()

    ids_row = cluster_ref[...]
    ids = jnp.transpose(jnp.broadcast_to(ids_row, (LANES, rows)))[:, 0:1]
    earlier = (ids == ids_row) & (iota((rows, rows), 0) < iota((rows, rows), 1))
    slot = jnp.sum(jnp.where(earlier, 1, 0), axis=0, keepdims=True)
    flat = ids_row * SLOTS + slot
    flat_ref[...] = jnp.broadcast_to(flat, flat_ref.shape)
    for s in range(SLOTS):
        select_ref[s] = jnp.where(chosen(flat, clusters, s), 1.0, 0.0).astype(BF16)

    def put(k, block):
        wide_ref[pl.ds(k, clusters, stride=depth), :] = block

    held = jnp.where(chosen(flat, clusters, me), priority_ref[...] - sentinel, 0)
    rank = jnp.sum(held, axis=1, keepdims=True) + sentinel
    rank = jnp.broadcast_to(rank, (clusters, LANES))
    put(depth - 2, (rank // RANK_BASE).astype(F32))
    put(depth - 1, (rank % RANK_BASE).astype(F32))

    mine = select_ref[me]
    square_ref[...] = jnp.zeros_like(square_ref)
    for j in range(COLUMN_PARTS):
        x_copies[j].wait()
        for k in range(j * part // LANES, (j + 1) * part // LANES, 2):
            picked = jnp.dot(mine, x_ref[:, k * LANES : (k + 2) * LANES], preferred_element_type=F32)
            put(k, picked[:, :LANES])
            put(k + 1, picked[:, LANES:])
        for r in range(0, rows, 128):
            total = square_ref[r : r + 128, :]
            for k in range(j * part // LANES, (j + 1) * part // LANES):
                block = x_ref[r : r + 128, k * LANES : (k + 1) * LANES].astype(F32)
                total = total + block * block
            square_ref[r : r + 128, :] = total

    gain = gain_ref[...].astype(F32)
    scale = lax.rsqrt(jnp.sum(square_ref[...], axis=1, keepdims=True) / width + 1e-05)
    for k in range(blocks(width)):
        cols = slice(k * LANES, (k + 1) * LANES)
        x_ref[:, cols] = (x_ref[:, cols].astype(F32) * scale * gain[k : k + 1, :]).astype(BF16)
    weight_copy.wait()
    values = jnp.dot(x_ref[...], weight_ref[...], preferred_element_type=F32).astype(BF16)
    pairs = blocks(weight_ref.shape[1])
    for s in range(SLOTS):
        picked = jnp.dot(select_ref[s], values, preferred_element_type=F32)
        for h in range(pairs):
            put(blocks(width) + s * pairs + h, picked[:, h * LANES : (h + 1) * LANES])

    share = wide_ref.shape[0] // ROW_PARTS
    out_copies = []
    for q in range(ROW_PARTS):
        span = pl.ds(q * share, share)
        message_ref[span, :] = wide_ref[span, :].astype(BF16)
        copy = pltpu.make_async_copy(message_ref.at[span, :], message_hbm.at[span, :], out_sems.at[q])
        copy.start()
        out_copies.append(copy)
    for copy in out_copies:
        copy.wait()


def pack(me, cluster, priority, gain, x, weight, clusters, depth):
    rows, width = x.shape
    vmem = pl.BlockSpec(memory_space=pltpu.VMEM)
    hbm = pl.BlockSpec(memory_space=pl.ANY)
    return pl.pallas_call(
        pack_kernel,
        in_specs=[pl.BlockSpec(memory_space=pltpu.SMEM), vmem, vmem, vmem, hbm, hbm],
        out_specs=[vmem, hbm],
        out_shape=[
            jax.ShapeDtypeStruct((8, rows), jnp.int32),
            jax.ShapeDtypeStruct((clusters * depth, LANES), BF16),
        ],
        scratch_shapes=[
            pltpu.VMEM((rows, width), BF16),
            pltpu.VMEM(weight.shape, BF16),
            pltpu.VMEM((clusters * depth, LANES), F32),
            pltpu.VMEM((clusters * depth, LANES), BF16),
            pltpu.VMEM((SLOTS, clusters, rows), BF16),
            pltpu.VMEM((rows, LANES), F32),
            pltpu.SemaphoreType.DMA((COLUMN_PARTS + 1,)),
            pltpu.SemaphoreType.DMA((ROW_PARTS,)),
        ],
        compiler_params=pltpu.CompilerParams(vmem_limit_bytes=56 * MIB),
        cost_estimate=pl.CostEstimate(
            flops=6 * clusters * rows * width, bytes_accessed=4 * rows * width, transcendentals=0
        ),
        name="pack",
    )(me, cluster, priority, gain, x, weight)


def owner_kernel(
    me_ref, got_hbm, w0, w1, w2a, w2b, w3a, w3b, out_ref,
    got_ref, wide_ref, weight_ref, mix_ref, value_ref, high, low, got_sems, weight_sems,
):
    clusters, width = high.shape
    depth = got_ref.shape[0] // clusters
    splits = SLOTS
    docs = clusters // splits
    kv_part = w0.shape[0]
    half = w2a.shape[0]
    pairs = blocks(kv_part)
    me = me_ref[0]
    share = got_ref.shape[0] // ROW_PARTS
    part = width // COLUMN_PARTS
    got_copies = []
    for q in range(ROW_PARTS):
        span = pl.ds(q * share, share)
        copy = pltpu.make_async_copy(got_hbm.at[span, :], got_ref.at[span, :], got_sems.at[q])
        copy.start()
        got_copies.append(copy)
    weight_copies = []
    for j in range(COLUMN_PARTS):
        cols = pl.ds(j * part, part)
        group = []
        for n, (source, other, shift) in enumerate(
            ((w0, 0, 0), (w1, 1, 0), (w2a, 2, 0), (w2b, 2, half), (w3a, 3, 0), (w3b, 3, half))
        ):
            start = pl.multiple_of((me ^ other) * kv_part + shift, half)
            copy = pltpu.make_async_copy(
                source.at[:, cols], weight_ref.at[pl.ds(start, source.shape[0]), cols], weight_sems.at[j, n]
            )
            copy.start()
            group.append(copy)
        weight_copies.append(group)

    for q in range(ROW_PARTS):
        span = pl.ds(q * share, share)
        got_copies[q].wait()
        wide_ref[span, :] = got_ref[span, :].astype(F32)
    for t in range(splits):
        for h in range(pairs):
            n = t * pairs + h
            for s in range(SLOTS):
                start = t * depth + blocks(width) + s * pairs + h
                piece = wide_ref[pl.ds(start, docs, stride=splits * depth), :]
                mix_ref[pl.ds(n * clusters + s, docs, stride=SLOTS), :] = piece
            value_ref[:, n * LANES : (n + 1) * LANES] = mix_ref[n * clusters : (n + 1) * clusters, :].astype(BF16)

    values = value_ref[...]
    for j in range(COLUMN_PARTS):
        for copy in weight_copies[j]:
            copy.wait()
        for k in range(j * part // LANES, (j + 1) * part // LANES, 2):
            cols = slice(k * LANES, (k + 2) * LANES)
            left = wide_ref[pl.ds(k, clusters, stride=depth), :]
            right = wide_ref[pl.ds(k + 1, clusters, stride=depth), :]
            hidden = jnp.concatenate([left, right], axis=1) + jnp.dot(
                values, weight_ref[:, cols], preferred_element_type=F32
            )
            upper = hidden.astype(BF16)
            high[:, cols] = upper
            low[:, cols] = (hidden - upper.astype(F32)).astype(BF16)
    contract = (((1,), (1,)), ((), ()))
    gram = lax.dot_general(high[...], high[...], contract, preferred_element_type=F32)
    cross = lax.dot_general(high[...], low[...], contract, preferred_element_type=F32)

    total = gram + (cross + jnp.transpose(cross))
    size = (clusters, clusters)
    diagonal = jnp.where(iota(size, 0) == iota(size, 1), total, 0.0)
    inv_col = lax.rsqrt(jnp.sum(diagonal, axis=1, keepdims=True) + 1e-06)
    inv_row = lax.rsqrt(jnp.sum(diagonal, axis=0, keepdims=True) + 1e-06)
    similarity = total * inv_col * inv_row
    rank = wide_ref[pl.ds(depth - 2, clusters, stride=depth), :] * RANK_BASE
    rank = rank + wide_ref[pl.ds(depth - 1, clusters, stride=depth), :]
    rank_row = jnp.transpose(rank)[0:1, :]
    allowed = rank[:, 0:1] < rank_row
    best = jnp.max(jnp.where(allowed, similarity, -2.0), axis=0, keepdims=True)
    best = jnp.maximum(best, -1.0)
    lane = iota(out_ref.shape, 1)
    result = jnp.zeros(out_ref.shape, F32)
    for s in range(SLOTS):
        wanted = (iota(size, 0) // SLOTS) * SLOTS + s
        mine = jnp.max(jnp.where(iota(size, 1) == wanted, best, -4.0), axis=1, keepdims=True)
        result = jnp.where(lane == s, mine, result)
    out_ref[...] = result


def owner_best(me, got, weights, clusters, width):
    depth = got.shape[0] // clusters
    kv_width = SLOTS * weights[0].shape[0]
    hbm = pl.BlockSpec(memory_space=pl.ANY)
    return pl.pallas_call(
        owner_kernel,
        in_specs=[pl.BlockSpec(memory_space=pltpu.SMEM), hbm] + [hbm] * len(weights),
        out_specs=pl.BlockSpec(memory_space=pltpu.VMEM),
        out_shape=jax.ShapeDtypeStruct((clusters, LANES), F32),
        scratch_shapes=[
            pltpu.VMEM(got.shape, BF16),
            pltpu.VMEM(got.shape, F32),
            pltpu.VMEM((kv_width, width), BF16),
            pltpu.VMEM((kv_width // LANES * clusters, LANES), F32),
            pltpu.VMEM((clusters, kv_width), BF16),
            pltpu.VMEM((clusters, width), BF16),
            pltpu.VMEM((clusters, width), BF16),
            pltpu.SemaphoreType.DMA((ROW_PARTS,)),
            pltpu.SemaphoreType.DMA((COLUMN_PARTS, len(weights))),
        ],
        compiler_params=pltpu.CompilerParams(vmem_limit_bytes=56 * MIB),
        cost_estimate=pl.CostEstimate(
            flops=4 * clusters * kv_width * width, bytes_accessed=12 * MIB, transcendentals=0
        ),
        name="owner_best",
    )(me, got, *weights)


def pick_kernel(flat_ref, best_ref, out_ref):
    clusters = best_ref.shape[0]
    flat = flat_ref[0:1, :]
    result = jnp.zeros((1, flat.shape[1]), F32)
    for s in range(SLOTS):
        held = jnp.where(chosen(flat, clusters, s), best_ref[:, s : s + 1], 0.0)
        result = result + jnp.sum(held, axis=0, keepdims=True)
    out_ref[...] = result


def pick(flat, best):
    vmem = pl.BlockSpec(memory_space=pltpu.VMEM)
    return pl.pallas_call(
        pick_kernel,
        in_specs=[vmem, vmem],
        out_specs=vmem,
        out_shape=jax.ShapeDtypeStruct((1, flat.shape[1]), F32),
        name="pick",
    )(flat, best)


def ring_pairs(splits, owners, way):
    cores = 2
    low = splits // cores
    length = 2 * low
    pairs = []
    for d in range(owners):
        for t in range(splits):
            x = (d % 2) * low + t // cores
            to = (x + way) % length
            other = (d // 2 * 2 + to // low) * splits + (to % low) * cores + t % cores
            pairs.append((d * splits + t, other))
    return pairs


def spread_weights(folded, splits, owners):
    half = folded.shape[0] // 2
    swap = [(t, t ^ 1) for t in range(splits)]
    first = lax.ppermute(folded[:half], AXES, ring_pairs(splits, owners, 1))
    second = lax.ppermute(folded[half:], AXES, ring_pairs(splits, owners, -1))
    beside = lax.ppermute(folded, "tensor", swap)
    return [folded, beside, first, second, lax.ppermute(first, "tensor", swap), lax.ppermute(second, "tensor", swap)]


def shards(final_input, norm_gain, value_weight, out_weight, cluster, priority):
    rows, width = final_input.shape
    splits = lax.axis_size("tensor")
    owners = lax.axis_size("dp")
    clusters = splits * owners
    me = jnp.stack([lax.axis_index("tensor").astype(jnp.int32), jnp.int32(owners * rows)])
    depth = blocks(width) + SLOTS * blocks(value_weight.shape[1]) + 2
    flat, message = pack(
        me,
        cluster.reshape(1, rows),
        priority.reshape(1, rows),
        norm_gain.reshape(blocks(width), LANES),
        final_input,
        value_weight,
        clusters,
        depth,
    )
    got = lax.all_to_all(message.reshape(clusters, depth // 2, 2, LANES), AXES, 0, 0, tiled=True)
    got = got.reshape(clusters * depth, LANES)
    kv_local = value_weight.shape[1] // HEAD_DIM
    group = HEADS // KV_HEADS
    out_weight, _ = lax.optimization_barrier((out_weight, flat))
    folded = jnp.sum(out_weight.reshape(kv_local, group, HEAD_DIM, width).astype(F32), axis=1)
    folded = folded.reshape(kv_local * HEAD_DIM, width).astype(BF16)
    weights = spread_weights(folded, splits, owners)
    best = owner_best(me, got, weights, clusters, width)
    returned = lax.all_to_all(best, AXES, 0, 0, tiled=True)
    return pick(flat, returned).reshape(rows)


def solution(mesh):
    in_specs = (P("dp", None), P(), P(None, "tensor"), P("tensor", None), P("dp", None), P("dp"))
    return jax.shard_map(shards, mesh=mesh, in_specs=in_specs, out_specs=P("dp"), check_vma=False)
```

time: 388 us -> 128 us (0.33)
  blocking collectives: 126 us -> 20.6 us
  waiting for transfers between devices: 135 us -> 53 us
  local copies, waits for them, and re-layouts: 61.1 us -> 1.14 us
  Pallas kernels: 0 us -> 24.1 us
  matrix products: 17.1 us -> 0 us
  other arithmetic: 22.6 us -> 5.75 us
  between operations: 13.5 us -> 0.06 us
  starting transfers between devices: 12.4 us -> 23.2 us
    psum x2 -> x0, waiting for transfers between devices: 123 us -> none  [the longest x1 100 us: shards(): lax.psum(partial_out.astype(jnp.bfloat16), 'tensor').astype(jnp.float32)]
    all_to_all x2 -> x1, blocking collectives: 126 us -> 20.6 us  [shards(): returned = lax.all_to_all(best, AXES, 0, 0, tiled=True)]
    ppermute x0 -> x5, waiting for transfers between devices: none -> 43.4 us  [the longest x1 37.8 us: spread_weights(): second = lax.ppermute(folded[half:], AXES, ring_pairs(splits, owners, -1))]
    reshape x4 -> x0, local copies, waits for them, and re-layouts: 34.8 us -> none  [the longest x1 29.3 us: tile_products(): return products.reshape(number_items, slot_count, slot_count)]
    pallas_call x0 -> x3, Pallas kernels: none -> 24.1 us  [the longest x1 11.5 us: owner_best(): pl.pallas_call(owner_kernel, in_specs=[pl.BlockSpec(memory_space=pltpu.SM...]
    dot_general x4 -> x0, matrix products: 17.1 us -> none  [the longest x1 11.3 us: tile_products(): jnp.einsum('acbf,ecdf->cabed', members, members, precision=lax.Precision....]
    dot_general x1 -> x0, local copies, waits for them, and re-layouts: 17.1 us -> none  [tile_products(): jnp.einsum('acbf,ecdf->cabed', members, members, precision=lax.Precision....]
    reduce_sum x4 -> x1, other arithmetic: 14.7 us -> 5.14 us  [shards(): jnp.sum(out_weight.reshape(kv_local, group, HEAD_DIM, width).astype(F32),...]
  transfers between devices with their start and end apart: 3 -> 6, of which waited for: 3 -> 4; matrix products, arithmetic and copies ran while one was open for 1% -> 4% of each run, Pallas kernels for 0% -> 0%
where the time goes in v1:
time: 128 us
  waiting for transfers between devices  53 us (41%)
  Pallas kernels  24.1 us (19%)
  starting transfers between devices  23.2 us (18%)
  blocking collectives  20.6 us (16%)
  other arithmetic  5.75 us (4%)
    ppermute x1, waiting for transfers between devices, spread_weights(): second = lax.ppermute(folded[half:], AXES, ring_pairs(splits, owners, -1))  37.8 us
    all_to_all x1, blocking collectives, shards(): returned = lax.all_to_all(best, AXES, 0, 0, tiled=True)  20.6 us
    all_to_all x1, starting transfers between devices, shards(): lax.all_to_all(message.reshape(clusters, depth // 2, 2, LANES), AXES, 0,...  16.5 us
    pallas_call x1, Pallas kernels, owner_best(): pl.pallas_call(owner_kernel, in_specs=[pl.BlockSpec(memory_space=pltpu.SM...  11.5 us
    pallas_call x1, Pallas kernels, pack(): pl.pallas_call(pack_kernel, in_specs=[pl.BlockSpec(memory_space=pltpu.SME...  10.6 us
    all_to_all x1, waiting for transfers between devices, shards(): lax.all_to_all(message.reshape(clusters, depth // 2, 2, LANES), AXES, 0,...  9.55 us
    reduce_sum x1, other arithmetic, shards(): jnp.sum(out_weight.reshape(kv_local, group, HEAD_DIM, width).astype(F32),...  5.14 us
    ppermute x1, waiting for transfers between devices, spread_weights(): first = lax.ppermute(folded[:half], AXES, ring_pairs(splits, owners, 1))  3.34 us
  transfers between devices with their start and end apart: 6, of which 4 were waited for; matrix products, arithmetic and copies ran while one was open for 4% of the time, Pallas kernels for 0%

profile of v1, /device:TPU:1, one launch (start us, length us, event | category | flops | bytes accessed | tf_op | source)
XLA Modules:
  0.0 127.8 jit_solution(12568773481393004331)
XLA Ops:
  0.0 0.6 pad_add_fusion.me_ref
  0.6 10.6 %pack.1 = (s32[8,512]{1,0:T(8,128)}, bf16[10752,128]{1,0:T(8,128)(2,1)}) custom-call(s32[2]{0:T(128)} %pad_add_fusion.me_ref, s32[1,512]{1,0:T(1,128)} %bitcast.24, s32[1,512]{1,0:T(1,128)} %bitcast.25, bf16[32,128]{1,0:T(8,128)(2,1)} %bitcast.23, bf16[512,4096]{1,0:T(8,128)(2,1)} %x_hbm.1, bf16[4096,256]{1,0:T(8,128)(2,1)} %weight_hbm.1), custom_call_target="tpu_custom_call" | custom-call | flops 3221225472 | bytes 8388608 | tf_op jit(solution)/shard_map/pack/pallas_call | solution.py:118
  11.2 16.5 %all-to-all-start = ((bf16[256,21,2,128]{3,2,1,0:T(2,128)(2,1)}), bf16[256,21,2,128]{3,2,1,0:T(2,128)(2,1)}, u32[]{:S(2)}, u32[]{:S(2)}) async-start(bf16[256,21,2,128]{3,2,1,0:T(2,128)(2,1)} %bitcast.20), calls=%async_computation | async-start | bytes 5505024 | tf_op jit(solution)/shard_map/all_to_all | solution.py:320
  27.8 5.1 %reduce = bf16[2,128,4096]{2,1,0:T(8,128)(2,1)S(1)} reduce(bf16[2,4,128,4096]{3,2,1,0:T(8,128)(2,1)} %bitcast.17, bf16[]{:T(256)} %constant.8), dimensions={1}, to_apply=%region_0.0.clone | reduce | flops 3145728 | bytes 10485762 | tf_op jit(solution)/shard_map/reduce_sum | solution.py:325
  33.0 0.0 copy-start
  33.0 0.1 slice_bitcast_fusion
  33.1 2.7 %collective-permute-start.2 = (bf16[128,4096]{1,0:T(8,128)(2,1)S(1)}, bf16[128,4096]{1,0:T(8,128)(2,1)S(1)}, u32[]{:S(2)}, u32[]{:S(2)}) collective-permute-start(bf16[128,4096]{1,0:T(8,128)(2,1)S(1)} %get-tuple-element.11), channel_id=1, source_target_pairs={{0,6},{1,7},{2,0},{3,1},{4,2},{5,3},{6,4},{7,5},{8,14},{9,15},{10,... | collective-permute-start | bytes 3145736 | tf_op jit(solution)/shard_map/ppermute | solution.py:298
  35.8 0.0 collective-permute-start.1
  35.8 1.6 %collective-permute-start = (bf16[256,4096]{1,0:T(8,128)(2,1)S(1)}, bf16[256,4096]{1,0:T(8,128)(2,1)}, u32[]{:S(2)}, u32[]{:S(2)}) collective-permute-start(bf16[256,4096]{1,0:T(8,128)(2,1)S(1)} %bitcast.18), channel_id=1, source_target_pairs={{0,1},{1,0},{2,3},{3,2},{4,5},{5,4},{6,7},{7,6},{8,9},{9,8},{10,11... | collective-permute-start | bytes 6291464 | tf_op jit(solution)/shard_map/ppermute | solution.py:299
  37.4 37.8 %collective-permute-done.2.w2b = bf16[128,4096]{1,0:T(8,128)(2,1)S(1)} collective-permute-done((bf16[128,4096]{1,0:T(8,128)(2,1)S(1)}, bf16[128,4096]{1,0:T(8,128)(2,1)S(1)}, u32[]{:S(2)}, u32[]{:S(2)}) %collective-permute-start.2) | collective-permute-done | bytes 1048608 | tf_op jit(solution)/shard_map/ppermute | solution.py:298
  75.2 0.0 copy-start.1
  75.2 1.3 collective-permute-start.4
  76.5 3.3 %collective-permute-done.1.w2a = bf16[128,4096]{1,0:T(8,128)(2,1)S(1)} collective-permute-done((bf16[128,4096]{1,0:T(8,128)(2,1)S(1)}, bf16[128,4096]{1,0:T(8,128)(2,1)S(1)}, u32[]{:S(2)}, u32[]{:S(2)}) %collective-permute-start.1) | collective-permute-done | bytes 1048608 | tf_op jit(solution)/shard_map/ppermute | solution.py:297
  79.8 0.0 copy-start.2
  79.8 1.1 collective-permute-start.3
  81.0 0.0 collective-permute-done.4.w3b
  81.0 0.0 copy-done.2
  81.0 0.0 copy-start.3
  81.0 2.3 %collective-permute-done.3.w3a = bf16[128,4096]{1,0:T(8,128)(2,1)S(1)} collective-permute-done((bf16[128,4096]{1,0:T(8,128)(2,1)S(1)}, bf16[128,4096]{1,0:T(8,128)(2,1)S(1)}, u32[]{:S(2)}, u32[]{:S(2)}) %collective-permute-start.3) | collective-permute-done | bytes 1048608 | tf_op jit(solution)/shard_map/ppermute | solution.py:300
  83.2 0.0 copy-done.3
  83.2 0.0 copy-start.4
  83.3 1.0 copy-done.4
  84.2 0.0 collective-permute-done.w1
  84.2 9.5 %all-to-all-done = bf16[256,21,2,128]{3,2,1,0:T(2,128)(2,1)} async-done(((bf16[256,21,2,128]{3,2,1,0:T(2,128)(2,1)}), bf16[256,21,2,128]{3,2,1,0:T(2,128)(2,1)}, u32[]{:S(2)}, u32[]{:S(2)}) %all-to-all-start) | async-done | bytes 2752544 | tf_op jit(solution)/shard_map/all_to_all | solution.py:320
  93.8 0.0 copy-done
  93.8 0.0 copy-done.1
  93.8 11.5 %owner_best.1 = f32[256,128]{1,0:T(8,128)} custom-call(s32[2]{0:T(128)} %pad_add_fusion.me_ref, bf16[10752,128]{1,0:T(8,128)(2,1)} %bitcast.5.got_hbm, bf16[256,4096]{1,0:T(8,128)(2,1)} %bitcast.19, bf16[256,4096]{1,0:T(8,128)(2,1)} %collective-permute-done.w1, bf16[128,4096]{1,0:T(8,128)(2,1)} %copy-done.2, bf16[128,4096]{1,0:T(8,128)(2,1)} %copy-done.1, ...), custom_call_target="tpu_custom_call" | custom-call | flops 4294967296 | bytes 12582912 | tf_op jit(solution)/shard_map/owner_best/pallas_call | solution.py:235
  105.4 20.6 %all_to_all.16 = f32[256,1,128]{2,1,0:T(1,128)} all-to-all(f32[256,1,128]{2,1,0:T(1,128)} %bitcast.22), channel_id=1, replica_groups=mesh['dp'=64,'tensor'=4] {'dp','tensor'}, dimensions={0} | all-to-all | bytes 262144 | tf_op jit(solution)/shard_map/all_to_all | solution.py:329
  126.0 1.9 %pick.1 = f32[1,512]{1,0:T(1,128)} custom-call(s32[8,512]{1,0:T(8,128)} %get-tuple-element.8.flat_ref, f32[256,128]{1,0:T(8,128)} %bitcast.21), custom_call_target="tpu_custom_call" | custom-call | tf_op jit(solution)/shard_map/pick/pallas_call | solution.py:271
Async XLA Ops:
  11.2 82.5 %all-to-all-start = ((bf16[256,21,2,128]{3,2,1,0:T(2,128)(2,1)}), bf16[256,21,2,128]{3,2,1,0:T(2,128)(2,1)}, u32[]{:S(2)}, u32[]{:S(2)}) async-start(bf16[256,21,2,128]{3,2,1,0:T(2,128)(2,1)} %bitcast.20), calls=%async_computation | async-start | bytes 5505024 | tf_op jit(solution)/shard_map/all_to_all | solution.py:320
  33.0 60.8 %copy-start = (bf16[2,128,4096]{2,1,0:T(8,128)(2,1)}, bf16[2,128,4096]{2,1,0:T(8,128)(2,1)S(1)}, u32[]{:S(2)}) copy-start(bf16[2,128,4096]{2,1,0:T(8,128)(2,1)S(1)} %reduce) | copy-start | bytes 6291460
  33.1 42.1 %collective-permute-start.2 = (bf16[128,4096]{1,0:T(8,128)(2,1)S(1)}, bf16[128,4096]{1,0:T(8,128)(2,1)S(1)}, u32[]{:S(2)}, u32[]{:S(2)}) collective-permute-start(bf16[128,4096]{1,0:T(8,128)(2,1)S(1)} %get-tuple-element.11), channel_id=1, source_target_pairs={{0,6},{1,7},{2,0},{3,1},{4,2},{5,3},{6,4},{7,5},{8,14},{9,15},{10,... | collective-permute-start | bytes 3145736 | tf_op jit(solution)/shard_map/ppermute | solution.py:298
  35.8 44.1 %collective-permute-start.1 = (bf16[128,4096]{1,0:T(8,128)(2,1)S(1)}, bf16[128,4096]{1,0:T(8,128)(2,1)S(1)}, u32[]{:S(2)}, u32[]{:S(2)}) collective-permute-start(bf16[128,4096]{1,0:T(8,128)(2,1)S(1)} %get-tuple-element.12), channel_id=1, source_target_pairs={{0,2},{1,3},{2,4},{3,5},{4,6},{5,7},{6,0},{7,1},{8,10},{9,11},{10,... | collective-permute-start | bytes 3145736 | tf_op jit(solution)/shard_map/ppermute | solution.py:297
  35.8 48.5 %collective-permute-start = (bf16[256,4096]{1,0:T(8,128)(2,1)S(1)}, bf16[256,4096]{1,0:T(8,128)(2,1)}, u32[]{:S(2)}, u32[]{:S(2)}) collective-permute-start(bf16[256,4096]{1,0:T(8,128)(2,1)S(1)} %bitcast.18), channel_id=1, source_target_pairs={{0,1},{1,0},{2,3},{3,2},{4,5},{5,4},{6,7},{7,6},{8,9},{9,8},{10,11... | collective-permute-start | bytes 6291464 | tf_op jit(solution)/shard_map/ppermute | solution.py:299
  75.2 18.6 %copy-start.1 = (bf16[128,4096]{1,0:T(8,128)(2,1)}, bf16[128,4096]{1,0:T(8,128)(2,1)S(1)}, u32[]{:S(2)}) copy-start(bf16[128,4096]{1,0:T(8,128)(2,1)S(1)} %collective-permute-done.2.w2b) | copy-start | bytes 3145732
  75.2 5.7 %collective-permute-start.4 = (bf16[128,4096]{1,0:T(8,128)(2,1)S(1)}, bf16[128,4096]{1,0:T(8,128)(2,1)S(1)}, u32[]{:S(2)}, u32[]{:S(2)}) collective-permute-start(bf16[128,4096]{1,0:T(8,128)(2,1)S(1)} %collective-permute-done.2.w2b), channel_id=1, source_target_pairs={{0,1},{1,0},{2,3},{3,2},{4,5},{5,4},{6,7},{7,6},{8,9},{9,8},{10,11... | collective-permute-start | bytes 3145736 | tf_op jit(solution)/shard_map/ppermute | solution.py:300
  79.8 1.1 copy-start.2
  79.8 3.4 %collective-permute-start.3 = (bf16[128,4096]{1,0:T(8,128)(2,1)S(1)}, bf16[128,4096]{1,0:T(8,128)(2,1)S(1)}, u32[]{:S(2)}, u32[]{:S(2)}) collective-permute-start(bf16[128,4096]{1,0:T(8,128)(2,1)S(1)} %collective-permute-done.1.w2a), channel_id=1, source_target_pairs={{0,1},{1,0},{2,3},{3,2},{4,5},{5,4},{6,7},{7,6},{8,9},{9,8},{10,11... | collective-permute-start | bytes 3145736 | tf_op jit(solution)/shard_map/ppermute | solution.py:300
  81.0 2.3 %copy-start.3 = (bf16[128,4096]{1,0:T(8,128)(2,1)}, bf16[128,4096]{1,0:T(8,128)(2,1)S(1)}, u32[]{:S(2)}) copy-start(bf16[128,4096]{1,0:T(8,128)(2,1)S(1)} %collective-permute-done.4.w3b) | copy-start | bytes 3145732
  83.2 1.0 copy-start.4

commit v2 on v1

v2 whole, which is shorter than its diff:
```python
import functools

import jax
import jax.numpy as jnp
from jax import lax
from jax.experimental import pallas as pl
from jax.experimental.pallas import tpu as pltpu
from jax.sharding import PartitionSpec as P

HEADS = 32
KV_HEADS = 8
HEAD_DIM = 128
SLOTS = 4
LANES = 128
AXES = ("dp", "tensor")
F32 = jnp.float32
BF16 = jnp.bfloat16
MIB = 2**20
COLUMN_PARTS = 2
ROW_PARTS = 4
OWNER_PARTS = 4
RANK_BASE = 128


def iota(shape, dim):
    return lax.broadcasted_iota(jnp.int32, shape, dim)


def chosen(flat_row, clusters, slot):
    rows = flat_row.shape[1]
    wanted = iota((clusters, rows), 0) * SLOTS + slot
    return flat_row == wanted


def blocks(width):
    return width // LANES


def pack_kernel(
    sentinel, cluster_ref, priority_ref, gain_ref, x_hbm, weight_hbm,
    flat_ref, message_ref,
    x_ref, weight_ref, scaled_ref, wide_ref, select_ref, square_ref, product_ref, in_sems,
):
    rows, width = x_ref.shape
    clusters = select_ref.shape[1]
    depth = wide_ref.shape[0] // clusters
    part = width // COLUMN_PARTS
    weight_copy = pltpu.make_async_copy(weight_hbm, weight_ref, in_sems.at[COLUMN_PARTS])
    weight_copy.start()
    x_copies = []
    for j in range(COLUMN_PARTS):
        cols = pl.ds(j * part, part)
        copy = pltpu.make_async_copy(x_hbm.at[:, cols], x_ref.at[:, cols], in_sems.at[j])
        copy.start()
        x_copies.append(copy)

    me = lax.axis_index("tensor").astype(jnp.int32)
    ids_row = cluster_ref[...]
    ids = jnp.transpose(jnp.broadcast_to(ids_row, (LANES, rows)))[:, 0:1]
    earlier = (ids == ids_row) & (iota((rows, rows), 0) < iota((rows, rows), 1))
    slot = jnp.sum(jnp.where(earlier, 1, 0), axis=0, keepdims=True)
    flat = ids_row * SLOTS + slot
    flat_ref[...] = jnp.broadcast_to(flat, flat_ref.shape)
    for s in range(SLOTS):
        select_ref[s] = jnp.where(chosen(flat, clusters, s), 1.0, 0.0).astype(BF16)

    def put(k, block):
        wide_ref[pl.ds(k, clusters, stride=depth), :] = block

    held = jnp.where(chosen(flat, clusters, me), priority_ref[...] - sentinel, 0)
    rank = jnp.sum(held, axis=1, keepdims=True) + sentinel
    rank = jnp.broadcast_to(rank, (clusters, LANES))
    put(depth - 2, (rank // RANK_BASE).astype(F32))
    put(depth - 1, (rank % RANK_BASE).astype(F32))

    weight_copy.wait()
    gain = jnp.transpose(gain_ref[...].astype(F32))
    for k in range(blocks(width)):
        span = slice(k * LANES, (k + 1) * LANES)
        scaled_ref[span, :] = (weight_ref[span, :].astype(F32) * gain[:, k : k + 1]).astype(BF16)

    mine = select_ref[me]
    square_ref[...] = jnp.zeros_like(square_ref)
    product_ref[...] = jnp.zeros_like(product_ref)
    for j in range(COLUMN_PARTS):
        x_copies[j].wait()
        for k in range(j * part // LANES, (j + 1) * part // LANES, 2):
            picked = jnp.dot(mine, x_ref[:, k * LANES : (k + 2) * LANES], preferred_element_type=F32)
            put(k, picked[:, :LANES])
            put(k + 1, picked[:, LANES:])
        span = slice(j * part, (j + 1) * part)
        product_ref[...] += jnp.dot(x_ref[:, span], scaled_ref[span, :], preferred_element_type=F32)
        for r in range(0, rows, 128):
            total = square_ref[r : r + 128, :]
            for k in range(j * part // LANES, (j + 1) * part // LANES):
                block = x_ref[r : r + 128, k * LANES : (k + 1) * LANES].astype(F32)
                total = total + block * block
            square_ref[r : r + 128, :] = total

    scale = lax.rsqrt(jnp.sum(square_ref[...], axis=1, keepdims=True) / width + 1e-05)
    values = (product_ref[...] * scale).astype(BF16)
    pairs = blocks(weight_ref.shape[1])
    for s in range(SLOTS):
        picked = jnp.dot(select_ref[s], values, preferred_element_type=F32)
        for h in range(pairs):
            put(blocks(width) + s * pairs + h, picked[:, h * LANES : (h + 1) * LANES])

    share = wide_ref.shape[0] // ROW_PARTS
    for q in range(ROW_PARTS):
        span = pl.ds(q * share, share)
        message_ref[span, :] = wide_ref[span, :].astype(BF16)


def pack(cluster, priority, gain, x, weight, clusters, depth, sentinel):
    rows, width = x.shape
    vmem = pl.BlockSpec(memory_space=pltpu.VMEM)
    hbm = pl.BlockSpec(memory_space=pl.ANY)
    return pl.pallas_call(
        functools.partial(pack_kernel, sentinel),
        in_specs=[vmem, vmem, vmem, hbm, hbm],
        out_specs=[vmem, vmem],
        out_shape=[
            jax.ShapeDtypeStruct((8, rows), jnp.int32),
            pltpu.VMEM((clusters * depth, LANES), BF16),
        ],
        scratch_shapes=[
            pltpu.VMEM((rows, width), BF16),
            pltpu.VMEM(weight.shape, BF16),
            pltpu.VMEM(weight.shape, BF16),
            pltpu.VMEM((clusters * depth, LANES), F32),
            pltpu.VMEM((SLOTS, clusters, rows), BF16),
            pltpu.VMEM((rows, LANES), F32),
            pltpu.VMEM((rows, weight.shape[1]), F32),
            pltpu.SemaphoreType.DMA((COLUMN_PARTS + 1,)),
        ],
        compiler_params=pltpu.CompilerParams(vmem_limit_bytes=58 * MIB),
        cost_estimate=pl.CostEstimate(
            flops=6 * clusters * rows * width, bytes_accessed=4 * rows * width, transcendentals=0
        ),
        name="pack",
    )(cluster, priority, gain, x, weight)


def owner_kernel(
    got_hbm, w0, w1, w2, w3, out_ref,
    got_ref, wide_ref, weight_ref, mix_ref, value_ref, high, low, gram_ref, cross_ref, got_sems, weight_sems,
):
    clusters, width = high.shape
    depth = got_ref.shape[0] // clusters
    splits = SLOTS
    docs = clusters // splits
    kv_part = w0.shape[0]
    pairs = blocks(kv_part)
    share = got_ref.shape[0] // ROW_PARTS
    got_copies = []
    for q in range(ROW_PARTS):
        span = pl.ds(q * share, share)
        copy = pltpu.make_async_copy(got_hbm.at[span, :], got_ref.at[span, :], got_sems.at[q])
        copy.start()
        got_copies.append(copy)
    me = lax.axis_index("tensor").astype(jnp.int32)
    part = width // OWNER_PARTS
    weight_copies = []
    for j in range(OWNER_PARTS):
        cols = pl.ds(j * part, part)
        group = []
        for n, source in enumerate((w0, w1, w2, w3)):
            start = pl.multiple_of((me ^ n) * kv_part, kv_part)
            group.append(
                pltpu.make_async_copy(
                    source.at[:, cols], weight_ref.at[pl.ds(start, kv_part), cols], weight_sems.at[j, n]
                )
            )
        weight_copies.append(group)

    def start_weights(j):
        for copy in weight_copies[j]:
            copy.start()

    start_weights(0)
    for q in range(ROW_PARTS):
        span = pl.ds(q * share, share)
        got_copies[q].wait()
        wide_ref[span, :] = got_ref[span, :].astype(F32)
    for j in range(1, OWNER_PARTS):
        start_weights(j)
    for t in range(splits):
        for h in range(pairs):
            n = t * pairs + h
            for s in range(SLOTS):
                start = t * depth + blocks(width) + s * pairs + h
                piece = wide_ref[pl.ds(start, docs, stride=splits * depth), :]
                mix_ref[pl.ds(n * clusters + s, docs, stride=SLOTS), :] = piece
            value_ref[:, n * LANES : (n + 1) * LANES] = mix_ref[n * clusters : (n + 1) * clusters, :].astype(BF16)

    values = value_ref[...]
    contract = (((1,), (1,)), ((), ()))
    for j in range(OWNER_PARTS):
        for copy in weight_copies[j]:
            copy.wait()
        for k in range(j * part // LANES, (j + 1) * part // LANES, 2):
            cols = slice(k * LANES, (k + 2) * LANES)
            left = wide_ref[pl.ds(k, clusters, stride=depth), :]
            right = wide_ref[pl.ds(k + 1, clusters, stride=depth), :]
            hidden = jnp.concatenate([left, right], axis=1) + jnp.dot(
                values, weight_ref[:, cols], preferred_element_type=F32
            )
            upper = hidden.astype(BF16)
            high[:, cols] = upper
            low[:, cols] = (hidden - upper.astype(F32)).astype(BF16)
        cols = slice(j * part, (j + 1) * part)
        gram = lax.dot_general(high[:, cols], high[:, cols], contract, preferred_element_type=F32)
        cross = lax.dot_general(high[:, cols], low[:, cols], contract, preferred_element_type=F32)
        gram_ref[...] = gram if j == 0 else gram_ref[...] + gram
        cross_ref[...] = cross if j == 0 else cross_ref[...] + cross

    gram = gram_ref[...]
    cross = cross_ref[...]
    total = gram + (cross + jnp.transpose(cross))
    size = (clusters, clusters)
    diagonal = jnp.where(iota(size, 0) == iota(size, 1), total, 0.0)
    inv_col = lax.rsqrt(jnp.sum(diagonal, axis=1, keepdims=True) + 1e-06)
    inv_row = lax.rsqrt(jnp.sum(diagonal, axis=0, keepdims=True) + 1e-06)
    similarity = total * inv_col * inv_row
    rank = wide_ref[pl.ds(depth - 2, clusters, stride=depth), :] * RANK_BASE
    rank = rank + wide_ref[pl.ds(depth - 1, clusters, stride=depth), :]
    rank_row = jnp.transpose(rank)[0:1, :]
    allowed = rank[:, 0:1] < rank_row
    best = jnp.max(jnp.where(allowed, similarity, -2.0), axis=0, keepdims=True)
    best = jnp.maximum(best, -1.0)
    lane = iota(out_ref.shape, 1)
    result = jnp.zeros(out_ref.shape, F32)
    for s in range(SLOTS):
        wanted = (iota(size, 0) // SLOTS) * SLOTS + s
        mine = jnp.max(jnp.where(iota(size, 1) == wanted, best, -4.0), axis=1, keepdims=True)
        result = jnp.where(lane == s, mine, result)
    out_ref[...] = result


def owner_best(got, weights, clusters):
    kv_part, width = weights[0].shape
    height = kv_part * len(weights)
    hbm = pl.BlockSpec(memory_space=pl.ANY)
    return pl.pallas_call(
        owner_kernel,
        in_specs=[hbm] * (1 + len(weights)),
        out_specs=pl.BlockSpec(memory_space=pltpu.VMEM),
        out_shape=jax.ShapeDtypeStruct((clusters, LANES), F32),
        scratch_shapes=[
            pltpu.VMEM(got.shape, BF16),
            pltpu.VMEM(got.shape, F32),
            pltpu.VMEM((height, width), BF16),
            pltpu.VMEM((height // LANES * clusters, LANES), F32),
            pltpu.VMEM((clusters, height), BF16),
            pltpu.VMEM((clusters, width), BF16),
            pltpu.VMEM((clusters, width), BF16),
            pltpu.VMEM((clusters, clusters), F32),
            pltpu.VMEM((clusters, clusters), F32),
            pltpu.SemaphoreType.DMA((ROW_PARTS,)),
            pltpu.SemaphoreType.DMA((OWNER_PARTS, len(weights))),
        ],
        compiler_params=pltpu.CompilerParams(vmem_limit_bytes=58 * MIB),
        cost_estimate=pl.CostEstimate(
            flops=4 * clusters * height * width, bytes_accessed=12 * MIB, transcendentals=0
        ),
        name="owner_best",
    )(got, *weights)


def pick_kernel(flat_ref, best_ref, out_ref):
    clusters = best_ref.shape[0]
    flat = flat_ref[0:1, :]
    result = jnp.zeros((1, flat.shape[1]), F32)
    for s in range(SLOTS):
        held = jnp.where(chosen(flat, clusters, s), best_ref[:, s : s + 1], 0.0)
        result = result + jnp.sum(held, axis=0, keepdims=True)
    out_ref[...] = result


def pick(flat, best):
    vmem = pl.BlockSpec(memory_space=pltpu.VMEM)
    return pl.pallas_call(
        pick_kernel,
        in_specs=[vmem, vmem],
        out_specs=vmem,
        out_shape=jax.ShapeDtypeStruct((1, flat.shape[1]), F32),
        name="pick",
    )(flat, best)


def ring_pairs(splits, owners):
    cores = 2
    low = splits // cores
    length = 2 * low
    pairs = []
    for d in range(owners):
        for t in range(splits):
            x = (d % 2) * low + t // cores
            to = (x + (1 if t % cores == 0 else -1)) % length
            other = (d // 2 * 2 + to // low) * splits + (to % low) * cores + t % cores
            pairs.append((d * splits + t, other))
    return pairs


def spread(part, splits, owners):
    swap = [(t, t ^ 1) for t in range(splits)]
    across = lax.ppermute(part, AXES, ring_pairs(splits, owners))
    return [part, lax.ppermute(part, "tensor", swap), across, lax.ppermute(across, "tensor", swap)]


def shards(final_input, norm_gain, value_weight, out_weight, cluster, priority):
    rows, width = final_input.shape
    splits = lax.axis_size("tensor")
    owners = lax.axis_size("dp")
    clusters = splits * owners
    depth = blocks(width) + SLOTS * blocks(value_weight.shape[1]) + 2
    flat, message = pack(
        cluster.reshape(1, rows),
        priority.reshape(1, rows),
        norm_gain.reshape(blocks(width), LANES),
        final_input,
        value_weight,
        clusters,
        depth,
        owners * rows,
    )
    got = lax.all_to_all(message.reshape(clusters, depth // 2, 2, LANES), AXES, 0, 0, tiled=True)
    got = got.reshape(clusters * depth, LANES)
    kv_local = value_weight.shape[1] // HEAD_DIM
    group = HEADS // KV_HEADS
    out_weight, _ = lax.optimization_barrier((out_weight, flat))
    folded = jnp.sum(out_weight.reshape(kv_local, group, HEAD_DIM, width).astype(F32), axis=1)
    folded = folded.reshape(kv_local * HEAD_DIM, width).astype(BF16)
    weights = spread(folded, splits, owners)
    best = owner_best(got, weights, clusters)
    returned = lax.all_to_all(best, AXES, 0, 0, tiled=True)
    return pick(flat, returned).reshape(rows)


def solution(mesh):
    in_specs = (P("dp", None), P(), P(None, "tensor"), P("tensor", None), P("dp", None), P("dp"))
    return jax.shard_map(shards, mesh=mesh, in_specs=in_specs, out_specs=P("dp"), check_vma=False)
```

time: 128 us -> 123 us (0.961)
  Pallas kernels: 24.1 us -> 18.3 us
  local copies, waits for them, and re-layouts: 1.14 us -> 2.92 us
  waiting for transfers between devices: 53 us -> 51.6 us
    pallas_call x2, Pallas kernels: 22.2 us -> 16.4 us  [the longest x1 8.7 us: pack(): pl.pallas_call(functools.partial(pack_kernel, sentinel), in_specs=[vmem,...]
    unnamed x10 -> x6, local copies, waits for them, and re-layouts: 1.01 us -> 2.92 us
    reduce_sum x1, other arithmetic: 5.14 us -> 6.91 us  [shards(): jnp.sum(out_weight.reshape(kv_local, group, HEAD_DIM, width).astype(F32),...]
    ppermute x5 -> x3, waiting for transfers between devices: 43.4 us -> 43.2 us  [the longest x1 40.6 us: spread(): across = lax.ppermute(part, AXES, ring_pairs(splits, owners))]
    ppermute x5 -> x3, starting transfers between devices: 6.69 us -> 6.91 us  [the longest x1 4.31 us: spread(): lax.ppermute(across, 'tensor', swap)]
  transfers between devices with their start and end apart: 6 -> 4, of which waited for: 4 -> 3; matrix products, arithmetic and copies ran while one was open for 4% -> 6% of each run, Pallas kernels for 0% -> 0%
where the time goes in v2:
time: 123 us
  waiting for transfers between devices  51.6 us (42%)
  starting transfers between devices  22.6 us (18%)
  blocking collectives  20.5 us (17%)
  Pallas kernels  18.3 us (15%)
  other arithmetic  6.91 us (6%)
  local copies, waits for them, and re-layouts  2.92 us (2%)
    ppermute x1, waiting for transfers between devices, spread(): across = lax.ppermute(part, AXES, ring_pairs(splits, owners))  40.6 us
    all_to_all x1, blocking collectives, shards(): returned = lax.all_to_all(best, AXES, 0, 0, tiled=True)  20.5 us
    all_to_all x1, starting transfers between devices, shards(): lax.all_to_all(message.reshape(clusters, depth // 2, 2, LANES), AXES, 0,...  15.7 us
    pallas_call x1, Pallas kernels, pack(): pl.pallas_call(functools.partial(pack_kernel, sentinel), in_specs=[vmem,...  8.7 us
    all_to_all x1, waiting for transfers between devices, shards(): lax.all_to_all(message.reshape(clusters, depth // 2, 2, LANES), AXES, 0,...  8.39 us
    pallas_call x1, Pallas kernels, owner_best(): pl.pallas_call(owner_kernel, in_specs=[hbm] * (1 + len(weights)), out_spe...  7.73 us
    reduce_sum x1, other arithmetic, shards(): jnp.sum(out_weight.reshape(kv_local, group, HEAD_DIM, width).astype(F32),...  6.91 us
    ppermute x1, starting transfers between devices, spread(): lax.ppermute(across, 'tensor', swap)  4.31 us
  transfers between devices with their start and end apart: 4, of which 3 were waited for; matrix products, arithmetic and copies ran while one was open for 6% of the time, Pallas kernels for 0%

profile of v2, /device:TPU:1, one launch (start us, length us, event | category | flops | bytes accessed | tf_op | source)
XLA Modules:
  0.0 122.8 jit_solution(13034957742778848657)
XLA Ops:
  0.0 8.7 %pack.1 = (s32[8,512]{1,0:T(8,128)}, bf16[10752,128]{1,0:T(8,128)(2,1)}) custom-call(s32[1,512]{1,0:T(1,128)} %bitcast.20, s32[1,512]{1,0:T(1,128)} %bitcast.21, bf16[32,128]{1,0:T(8,128)(2,1)} %bitcast.19, bf16[512,4096]{1,0:T(8,128)(2,1)} %x_hbm.1, bf16[4096,256]{1,0:T(8,128)(2,1)} %weight_hbm.1), custom_call_target="tpu_custom_call" | custom-call | flops 3221225472 | bytes 8388608 | tf_op jit(solution)/shard_map/pack/pallas_call | solution.py:118
  8.7 15.7 %all-to-all-start = ((bf16[256,21,2,128]{3,2,1,0:T(2,128)(2,1)}), bf16[256,21,2,128]{3,2,1,0:T(2,128)(2,1)S(1)}, u32[]{:S(2)}, u32[]{:S(2)}) async-start(bf16[256,21,2,128]{3,2,1,0:T(2,128)(2,1)} %bitcast.3), calls=%async_computation | async-start | bytes 5505024 | tf_op jit(solution)/shard_map/all_to_all | solution.py:327
  24.4 6.9 %reduce = bf16[2,128,4096]{2,1,0:T(8,128)(2,1)} reduce(bf16[2,4,128,4096]{3,2,1,0:T(8,128)(2,1)} %bitcast.12, bf16[]{:T(256)} %constant.2), dimensions={1}, to_apply=%region_0.0.clone | reduce | flops 3145728 | bytes 10485762 | tf_op jit(solution)/shard_map/reduce_sum | solution.py:332
  31.3 2.6 %collective-permute-start.1 = (bf16[256,4096]{1,0:T(8,128)(2,1)}, bf16[256,4096]{1,0:T(8,128)(2,1)S(1)}, u32[]{:S(2)}, u32[]{:S(2)}) collective-permute-start(bf16[256,4096]{1,0:T(8,128)(2,1)} %bitcast.14), channel_id=1, source_target_pairs={{0,2},{1,7},{2,4},{3,1},{4,6},{5,3},{6,0},{7,5},{8,10},{9,15},{10,... | collective-permute-start | bytes 6291464 | tf_op jit(solution)/shard_map/ppermute | solution.py:307
  33.9 0.0 collective-permute-start
  33.9 40.6 %collective-permute-done.1.w2 = bf16[256,4096]{1,0:T(8,128)(2,1)S(1)} collective-permute-done((bf16[256,4096]{1,0:T(8,128)(2,1)}, bf16[256,4096]{1,0:T(8,128)(2,1)S(1)}, u32[]{:S(2)}, u32[]{:S(2)}) %collective-permute-start.1) | collective-permute-done | bytes 2097184 | tf_op jit(solution)/shard_map/ppermute | solution.py:307
  74.5 0.0 copy-start.1
  74.5 4.3 %collective-permute-start.2 = (bf16[256,4096]{1,0:T(8,128)(2,1)S(1)}, bf16[256,4096]{1,0:T(8,128)(2,1)}, u32[]{:S(2)}, u32[]{:S(2)}) collective-permute-start(bf16[256,4096]{1,0:T(8,128)(2,1)S(1)} %collective-permute-done.1.w2), channel_id=1, source_target_pairs={{0,1},{1,0},{2,3},{3,2},{4,5},{5,4},{6,7},{7,6},{8,9},{9,8},{10,11... | collective-permute-start | bytes 6291464 | tf_op jit(solution)/shard_map/ppermute | solution.py:308
  78.8 0.0 collective-permute-done.w1
  78.8 0.0 copy-done.1
  78.8 0.0 copy-start.2
  78.8 1.4 %copy-done.2 = bf16[256,4096]{1,0:T(8,128)(2,1)} copy-done((bf16[256,4096]{1,0:T(8,128)(2,1)}, bf16[256,4096]{1,0:T(8,128)(2,1)S(1)}, u32[]{:S(2)}) %copy-start.2) | copy-done | bytes 2097176
  80.2 2.5 %collective-permute-done.2.w3 = bf16[256,4096]{1,0:T(8,128)(2,1)} collective-permute-done((bf16[256,4096]{1,0:T(8,128)(2,1)S(1)}, bf16[256,4096]{1,0:T(8,128)(2,1)}, u32[]{:S(2)}, u32[]{:S(2)}) %collective-permute-start.2) | collective-permute-done | bytes 2097184 | tf_op jit(solution)/shard_map/ppermute | solution.py:308
  82.8 8.4 %all-to-all-done = bf16[256,21,2,128]{3,2,1,0:T(2,128)(2,1)S(1)} async-done(((bf16[256,21,2,128]{3,2,1,0:T(2,128)(2,1)}), bf16[256,21,2,128]{3,2,1,0:T(2,128)(2,1)S(1)}, u32[]{:S(2)}, u32[]{:S(2)}) %all-to-all-start) | async-done | bytes 2752544 | tf_op jit(solution)/shard_map/all_to_all | solution.py:327
  91.1 0.0 copy-start
  91.1 1.5 %copy-done = bf16[256,21,2,128]{3,2,1,0:T(2,128)(2,1)} copy-done((bf16[256,21,2,128]{3,2,1,0:T(2,128)(2,1)}, bf16[256,21,2,128]{3,2,1,0:T(2,128)(2,1)S(1)}, u32[]{:S(2)}) %copy-start) | copy-done | bytes 2752536
  92.7 7.7 %owner_best.1 = f32[256,128]{1,0:T(8,128)} custom-call(bf16[10752,128]{1,0:T(8,128)(2,1)} %bitcast.13, bf16[256,4096]{1,0:T(8,128)(2,1)} %bitcast.16, bf16[256,4096]{1,0:T(8,128)(2,1)} %copy-done.2, bf16[256,4096]{1,0:T(8,128)(2,1)} %copy-done.1, bf16[256,4096]{1,0:T(8,128)(2,1)} %collective-permute-done.2.w3), custom_call_target="tpu_custom_call" | custom-call | flops 4294967296 | bytes 12582912 | tf_op jit(solution)/shard_map/owner_best/pallas_call | solution.py:244
  100.4 20.5 %all_to_all.16 = f32[256,1,128]{2,1,0:T(1,128)} all-to-all(f32[256,1,128]{2,1,0:T(1,128)} %bitcast.18), channel_id=1, replica_groups=mesh['dp'=64,'tensor'=4] {'dp','tensor'}, dimensions={0} | all-to-all | bytes 262144 | tf_op jit(solution)/shard_map/all_to_all | solution.py:336
  120.9 1.9 %pick.1 = f32[1,512]{1,0:T(1,128)} custom-call(s32[8,512]{1,0:T(8,128)} %get-tuple-element.8.flat_ref, f32[256,128]{1,0:T(8,128)} %bitcast.17), custom_call_target="tpu_custom_call" | custom-call | tf_op jit(solution)/shard_map/pick/pallas_call | solution.py:282
Async XLA Ops:
  8.7 82.4 %all-to-all-start = ((bf16[256,21,2,128]{3,2,1,0:T(2,128)(2,1)}), bf16[256,21,2,128]{3,2,1,0:T(2,128)(2,1)S(1)}, u32[]{:S(2)}, u32[]{:S(2)}) async-start(bf16[256,21,2,128]{3,2,1,0:T(2,128)(2,1)} %bitcast.3), calls=%async_computation | async-start | bytes 5505024 | tf_op jit(solution)/shard_map/all_to_all | solution.py:327
  31.3 43.2 %collective-permute-start.1 = (bf16[256,4096]{1,0:T(8,128)(2,1)}, bf16[256,4096]{1,0:T(8,128)(2,1)S(1)}, u32[]{:S(2)}, u32[]{:S(2)}) collective-permute-start(bf16[256,4096]{1,0:T(8,128)(2,1)} %bitcast.14), channel_id=1, source_target_pairs={{0,2},{1,7},{2,4},{3,1},{4,6},{5,3},{6,0},{7,5},{8,10},{9,15},{10,... | collective-permute-start | bytes 6291464 | tf_op jit(solution)/shard_map/ppermute | solution.py:307
  33.9 44.9 %collective-permute-start = (bf16[256,4096]{1,0:T(8,128)(2,1)}, bf16[256,4096]{1,0:T(8,128)(2,1)S(1)}, u32[]{:S(2)}, u32[]{:S(2)}) collective-permute-start(bf16[256,4096]{1,0:T(8,128)(2,1)} %bitcast.15), channel_id=1, source_target_pairs={{0,1},{1,0},{2,3},{3,2},{4,5},{5,4},{6,7},{7,6},{8,9},{9,8},{10,11... | collective-permute-start | bytes 6291464 | tf_op jit(solution)/shard_map/ppermute | solution.py:308
  74.5 4.3 %copy-start.1 = (bf16[256,4096]{1,0:T(8,128)(2,1)}, bf16[256,4096]{1,0:T(8,128)(2,1)S(1)}, u32[]{:S(2)}) copy-start(bf16[256,4096]{1,0:T(8,128)(2,1)S(1)} %collective-permute-done.1.w2) | copy-start | bytes 6291460
  74.5 8.2 %collective-permute-start.2 = (bf16[256,4096]{1,0:T(8,128)(2,1)S(1)}, bf16[256,4096]{1,0:T(8,128)(2,1)}, u32[]{:S(2)}, u32[]{:S(2)}) collective-permute-start(bf16[256,4096]{1,0:T(8,128)(2,1)S(1)} %collective-permute-done.1.w2), channel_id=1, source_target_pairs={{0,1},{1,0},{2,3},{3,2},{4,5},{5,4},{6,7},{7,6},{8,9},{9,8},{10,11... | collective-permute-start | bytes 6291464 | tf_op jit(solution)/shard_map/ppermute | solution.py:308
  78.8 1.4 %copy-start.2 = (bf16[256,4096]{1,0:T(8,128)(2,1)}, bf16[256,4096]{1,0:T(8,128)(2,1)S(1)}, u32[]{:S(2)}) copy-start(bf16[256,4096]{1,0:T(8,128)(2,1)S(1)} %collective-permute-done.w1) | copy-start | bytes 6291460
  91.1 1.5 %copy-start = (bf16[256,21,2,128]{3,2,1,0:T(2,128)(2,1)}, bf16[256,21,2,128]{3,2,1,0:T(2,128)(2,1)S(1)}, u32[]{:S(2)}) copy-start(bf16[256,21,2,128]{3,2,1,0:T(2,128)(2,1)S(1)} %all-to-all-done) | copy-start | bytes 8257540

commit v3 on v2

v3 whole, which is shorter than its diff:
```python
import functools

import jax
import jax.numpy as jnp
from jax import lax
from jax.experimental import pallas as pl
from jax.experimental.pallas import tpu as pltpu
from jax.sharding import PartitionSpec as P

HEADS = 32
KV_HEADS = 8
HEAD_DIM = 128
SLOTS = 4
LANES = 128
AXES = ("dp", "tensor")
F32 = jnp.float32
BF16 = jnp.bfloat16
MIB = 2**20
COLUMN_PARTS = 2
ROW_PARTS = 4
OWNER_PARTS = 4
PROJECT_PARTS = 4
AHEAD = 3
FOLD_PARTS = 8
RANK_BASE = 128


def iota(shape, dim):
    return lax.broadcasted_iota(jnp.int32, shape, dim)


def chosen(flat_row, clusters, slot):
    rows = flat_row.shape[1]
    wanted = iota((clusters, rows), 0) * SLOTS + slot
    return flat_row == wanted


def blocks(width):
    return width // LANES


def row_parity():
    return (lax.axis_index("dp").astype(jnp.int32) // 2) % 2


def pack_kernel(
    sentinel, cluster_ref, priority_ref, x_hbm, project_hbm, flat_ref, message_ref, half_hbm, x_ref, wide_ref, half_ref, sems,
):
    rows, width = x_ref.shape
    part = width // COLUMN_PARTS
    x_copies = []
    for j in range(COLUMN_PARTS):
        cols = pl.ds(j * part, part)
        copy = pltpu.make_async_copy(x_hbm.at[:, cols], x_ref.at[:, cols], sems.at[j])
        copy.start()
        x_copies.append(copy)
    half = half_hbm.shape[0]
    start = pl.multiple_of(row_parity() * half, half)
    half_in = pltpu.make_async_copy(project_hbm.at[pl.ds(start, half), :], half_ref, sems.at[COLUMN_PARTS])
    half_in.start()

    me = lax.axis_index("tensor").astype(jnp.int32)
    ids_row = cluster_ref[...]
    ids = jnp.transpose(jnp.broadcast_to(ids_row, (LANES, rows)))[:, 0:1]
    earlier = (ids == ids_row) & (iota((rows, rows), 0) < iota((rows, rows), 1))
    slot = jnp.sum(jnp.where(earlier, 1, 0), axis=0, keepdims=True)
    flat = ids_row * SLOTS + slot
    flat_ref[...] = jnp.broadcast_to(flat, flat_ref.shape)
    depth = blocks(width) + 2
    clusters = wide_ref.shape[0] // depth

    def put(k, block):
        wide_ref[pl.ds(k, clusters, stride=depth), :] = block

    mine = chosen(flat, clusters, me)
    held = jnp.where(mine, priority_ref[...] - sentinel, 0)
    rank = jnp.sum(held, axis=1, keepdims=True) + sentinel
    rank = jnp.broadcast_to(rank, (clusters, LANES))
    put(depth - 2, (rank // RANK_BASE).astype(F32))
    put(depth - 1, (rank % RANK_BASE).astype(F32))

    select = jnp.where(mine, 1.0, 0.0).astype(BF16)
    half_out = pltpu.make_async_copy(half_ref, half_hbm, sems.at[COLUMN_PARTS + 1])
    for j in range(COLUMN_PARTS):
        x_copies[j].wait()
        if j == COLUMN_PARTS - 1:
            half_in.wait()
            half_out.start()
        for k in range(j * part // LANES, (j + 1) * part // LANES, 2):
            picked = jnp.dot(select, x_ref[:, k * LANES : (k + 2) * LANES], preferred_element_type=F32)
            put(k, picked[:, :LANES])
            put(k + 1, picked[:, LANES:])

    share = wide_ref.shape[0] // ROW_PARTS
    for q in range(ROW_PARTS):
        span = pl.ds(q * share, share)
        message_ref[span, :] = wide_ref[span, :].astype(BF16)
    half_out.wait()


def pack(cluster, priority, x, project, clusters, depth, sentinel):
    rows, width = x.shape
    hbm = pl.BlockSpec(memory_space=pl.ANY)
    vmem = pl.BlockSpec(memory_space=pltpu.VMEM)
    return pl.pallas_call(
        functools.partial(pack_kernel, sentinel),
        in_specs=[vmem, vmem, hbm, hbm],
        out_specs=[vmem, vmem, hbm],
        out_shape=[
            jax.ShapeDtypeStruct((8, rows), jnp.int32),
            pltpu.VMEM((clusters * depth, LANES), BF16),
            jax.ShapeDtypeStruct((project.shape[0] // 2, project.shape[1]), BF16),
        ],
        scratch_shapes=[
            pltpu.VMEM((rows, width), BF16),
            pltpu.VMEM((clusters * depth, LANES), F32),
            pltpu.VMEM((project.shape[0] // 2, project.shape[1]), BF16),
            pltpu.SemaphoreType.DMA((COLUMN_PARTS + 2,)),
        ],
        compiler_params=pltpu.CompilerParams(vmem_limit_bytes=58 * MIB),
        cost_estimate=pl.CostEstimate(
            flops=2 * clusters * rows * width, bytes_accessed=3 * rows * width, transcendentals=0
        ),
        name="pack",
    )(cluster, priority, x, project)


def fold_kernel(weight_hbm, out_hbm, half_hbm, weight_ref, out_ref, in_sems, out_sems, half_sem):
    group = HEADS // KV_HEADS
    kv_part, width = out_ref.shape
    part = width // FOLD_PARTS
    in_copies = []
    for j in range(FOLD_PARTS):
        cols = pl.ds(j * part, part)
        copy = pltpu.make_async_copy(weight_hbm.at[:, cols], weight_ref.at[:, cols], in_sems.at[j])
        copy.start()
        in_copies.append(copy)
    out_copies = []
    for j in range(FOLD_PARTS):
        in_copies[j].wait()
        cols = slice(j * part, (j + 1) * part)
        for kv in range(kv_part // HEAD_DIM):
            total = 0.0
            for g in range(group):
                start = (kv * group + g) * HEAD_DIM
                total = total + weight_ref[start : start + HEAD_DIM, cols].astype(F32)
            out_ref[kv * HEAD_DIM : (kv + 1) * HEAD_DIM, cols] = total.astype(BF16)
        span = pl.ds(j * part, part)
        copy = pltpu.make_async_copy(out_ref.at[:, span], out_hbm.at[:, span], out_sems.at[j])
        copy.start()
        out_copies.append(copy)
    half = half_hbm.shape[0]
    start = pl.multiple_of(row_parity() * half, half)
    copy = pltpu.make_async_copy(out_ref.at[pl.ds(start, half), :], half_hbm, half_sem)
    copy.start()
    out_copies.append(copy)
    for copy in out_copies:
        copy.wait()


def fold(out_weight):
    height, width = out_weight.shape
    kv_part = height * KV_HEADS // HEADS
    hbm = pl.BlockSpec(memory_space=pl.ANY)
    return pl.pallas_call(
        fold_kernel,
        in_specs=[hbm],
        out_specs=[hbm, hbm],
        out_shape=[
            jax.ShapeDtypeStruct((kv_part, width), BF16),
            jax.ShapeDtypeStruct((kv_part // 2, width), BF16),
        ],
        scratch_shapes=[
            pltpu.VMEM(out_weight.shape, BF16),
            pltpu.VMEM((kv_part, width), BF16),
            pltpu.SemaphoreType.DMA((FOLD_PARTS,)),
            pltpu.SemaphoreType.DMA((FOLD_PARTS,)),
            pltpu.SemaphoreType.DMA,
        ],
        compiler_params=pltpu.CompilerParams(vmem_limit_bytes=58 * MIB),
        cost_estimate=pl.CostEstimate(flops=4 * 10**11, bytes_accessed=10 * MIB, transcendentals=0),
        name="fold",
    )(out_weight)


def owner_kernel(
    gain_ref, got_hbm, v0, v1, v2, v2y, v3, v3y, w0, w1, w2, w2y, w3, w3y, out_ref,
    got_ref, wide_ref, x_ref, gained_ref, project_ref, weight_ref, high, low, gram_ref, cross_ref, product_ref,
    got_sems, project_sems, weight_sems,
):
    clusters, width = high.shape
    depth = got_ref.shape[0] // clusters
    kv_part = w0.shape[0]
    share = got_ref.shape[0] // ROW_PARTS
    got_copies = []
    for q in range(ROW_PARTS):
        span = pl.ds(q * share, share)
        got_copies.append(pltpu.make_async_copy(got_hbm.at[span, :], got_ref.at[span, :], got_sems.at[q]))
    half = v2.shape[0]
    near = row_parity() * half
    far = half - near
    step = 2 * half // PROJECT_PARTS
    starts = []
    project_groups = []
    for p in range(PROJECT_PARTS):
        inner = p * step % half
        begin = pl.multiple_of((near if p * step < half else far) + inner, step)
        starts.append(begin)
        third, fourth = (v2, v3) if p * step < half else (v2y, v3y)
        project_groups.append(
            [
                pltpu.make_async_copy(
                    source.at[pl.ds(first, step), :],
                    project_ref.at[p, :, pl.ds(n * kv_part, kv_part)],
                    project_sems.at[p, n],
                )
                for n, (source, first) in enumerate(((v0, begin), (v1, begin), (third, inner), (fourth, inner)))
            ]
        )
    part = width // OWNER_PARTS
    rows = w2.shape[0]
    near = row_parity() * rows
    far = rows - near
    weight_groups = []
    for j in range(OWNER_PARTS):
        cols = pl.ds(j * part, part)
        group = []
        for i, (source, n, shift) in enumerate(
            ((w0, 0, 0), (w1, 1, 0), (w2, 2, near), (w2y, 2, far), (w3, 3, near), (w3y, 3, far))
        ):
            span = pl.ds(pl.multiple_of(n * kv_part + shift, rows), source.shape[0])
            group.append(
                pltpu.make_async_copy(source.at[:, cols], weight_ref.at[span, cols], weight_sems.at[j, i])
            )
        weight_groups.append(group)
    groups = project_groups + weight_groups

    def start(n):
        if n < len(groups):
            for copy in groups[n]:
                copy.start()

    for copy in got_copies:
        copy.start()
    for q in range(ROW_PARTS):
        span = pl.ds(q * share, share)
        got_copies[q].wait()
        if q >= ROW_PARTS - AHEAD:
            start(q - ROW_PARTS + AHEAD)
        wide_ref[span, :] = got_ref[span, :].astype(F32)
    gain = gain_ref[...].astype(F32)
    squares = jnp.zeros((clusters, LANES), F32)
    for k in range(blocks(width)):
        cols = slice(k * LANES, (k + 1) * LANES)
        block = wide_ref[pl.ds(k, clusters, stride=depth), :]
        squares = squares + block * block
        x_ref[:, cols] = block.astype(BF16)
        gained_ref[:, cols] = (block * gain[k : k + 1, :]).astype(BF16)
    for p in range(PROJECT_PARTS):
        for copy in project_groups[p]:
            copy.wait()
        start(p + AHEAD)
        product = jnp.dot(
            gained_ref[:, pl.ds(starts[p], step)], project_ref[p], preferred_element_type=F32
        )
        product_ref[...] = product if p == 0 else product_ref[...] + product
    scale = lax.rsqrt(jnp.sum(squares, axis=1, keepdims=True) / width + 1e-05)
    values = (product_ref[...] * scale).astype(BF16)
    contract = (((1,), (1,)), ((), ()))
    for j in range(OWNER_PARTS):
        for copy in weight_groups[j]:
            copy.wait()
        start(PROJECT_PARTS + j + AHEAD)
        for k in range(j * part // LANES, (j + 1) * part // LANES, 2):
            cols = slice(k * LANES, (k + 2) * LANES)
            hidden = x_ref[:, cols].astype(F32) + jnp.dot(
                values, weight_ref[:, cols], preferred_element_type=F32
            )
            upper = hidden.astype(BF16)
            high[:, cols] = upper
            low[:, cols] = (hidden - upper.astype(F32)).astype(BF16)
        cols = slice(j * part, (j + 1) * part)
        gram = lax.dot_general(high[:, cols], high[:, cols], contract, preferred_element_type=F32)
        cross = lax.dot_general(high[:, cols], low[:, cols], contract, preferred_element_type=F32)
        gram_ref[...] = gram if j == 0 else gram_ref[...] + gram
        cross_ref[...] = cross if j == 0 else cross_ref[...] + cross

    gram = gram_ref[...]
    cross = cross_ref[...]
    total = gram + (cross + jnp.transpose(cross))
    size = (clusters, clusters)
    diagonal = jnp.where(iota(size, 0) == iota(size, 1), total, 0.0)
    inv_col = lax.rsqrt(jnp.sum(diagonal, axis=1, keepdims=True) + 1e-06)
    inv_row = lax.rsqrt(jnp.sum(diagonal, axis=0, keepdims=True) + 1e-06)
    similarity = total * inv_col * inv_row
    rank = wide_ref[pl.ds(depth - 2, clusters, stride=depth), :] * RANK_BASE
    rank = rank + wide_ref[pl.ds(depth - 1, clusters, stride=depth), :]
    rank_row = jnp.transpose(rank)[0:1, :]
    allowed = rank[:, 0:1] < rank_row
    best = jnp.max(jnp.where(allowed, similarity, -2.0), axis=0, keepdims=True)
    best = jnp.maximum(best, -1.0)
    lane = iota(out_ref.shape, 1)
    result = jnp.zeros(out_ref.shape, F32)
    for s in range(SLOTS):
        wanted = (iota(size, 0) // SLOTS) * SLOTS + s
        mine = jnp.max(jnp.where(iota(size, 1) == wanted, best, -4.0), axis=1, keepdims=True)
        result = jnp.where(lane == s, mine, result)
    out_ref[...] = result


def owner_best(gain, got, projects, weights, clusters):
    kv_part, width = weights[0].shape
    height = kv_part * SLOTS
    hbm = pl.BlockSpec(memory_space=pl.ANY)
    vmem = pl.BlockSpec(memory_space=pltpu.VMEM)
    return pl.pallas_call(
        owner_kernel,
        in_specs=[vmem] + [hbm] * (1 + len(projects) + len(weights)),
        out_specs=vmem,
        out_shape=jax.ShapeDtypeStruct((clusters, LANES), F32),
        scratch_shapes=[
            pltpu.VMEM(got.shape, BF16),
            pltpu.VMEM(got.shape, F32),
            pltpu.VMEM((clusters, width), BF16),
            pltpu.VMEM((clusters, width), BF16),
            pltpu.VMEM((PROJECT_PARTS, width // PROJECT_PARTS, height), BF16),
            pltpu.VMEM((height, width), BF16),
            pltpu.VMEM((clusters, width), BF16),
            pltpu.VMEM((clusters, width), BF16),
            pltpu.VMEM((clusters, clusters), F32),
            pltpu.VMEM((clusters, clusters), F32),
            pltpu.VMEM((clusters, height), F32),
            pltpu.SemaphoreType.DMA((ROW_PARTS,)),
            pltpu.SemaphoreType.DMA((PROJECT_PARTS, SLOTS)),
            pltpu.SemaphoreType.DMA((OWNER_PARTS, len(weights))),
        ],
        compiler_params=pltpu.CompilerParams(vmem_limit_bytes=58 * MIB),
        cost_estimate=pl.CostEstimate(
            flops=6 * clusters * height * width, bytes_accessed=20 * MIB, transcendentals=0
        ),
        name="owner_best",
    )(gain, got, *projects, *weights)


def pick_kernel(flat_ref, best_ref, out_ref):
    clusters = best_ref.shape[0]
    flat = flat_ref[0:1, :]
    result = jnp.zeros((1, flat.shape[1]), F32)
    for s in range(SLOTS):
        held = jnp.where(chosen(flat, clusters, s), best_ref[:, s : s + 1], 0.0)
        result = result + jnp.sum(held, axis=0, keepdims=True)
    out_ref[...] = result


def pick(flat, best):
    vmem = pl.BlockSpec(memory_space=pltpu.VMEM)
    return pl.pallas_call(
        pick_kernel,
        in_specs=[vmem, vmem],
        out_specs=vmem,
        out_shape=jax.ShapeDtypeStruct((1, flat.shape[1]), F32),
        name="pick",
    )(flat, best)


def ring_pairs(splits, owners):
    cores = 2
    low = splits // cores
    length = 2 * low
    pairs = []
    for d in range(owners):
        for t in range(splits):
            x = (d % 2) * low + t // cores
            to = (x + (1 if t % cores == 0 else -1)) % length
            other = (d // 2 * 2 + to // low) * splits + (to % low) * cores + t % cores
            pairs.append((d * splits + t, other))
    return pairs


def column_pairs(splits, owners):
    pairs = []
    for d in range(owners):
        for t in range(splits):
            y = (d // 2) % 4
            to = (y + (1 if t % 2 == 0 else -1)) % 4
            pairs.append((d * splits + t, (d + (to - y) * 2) * splits + t))
    return pairs


def spread_halves(part, half, splits, owners):
    swap = [(t, t ^ 1) for t in range(splits)]
    near = lax.ppermute(half, AXES, ring_pairs(splits, owners))
    far = lax.ppermute(near, AXES, column_pairs(splits, owners))
    beside = lax.ppermute(part, "tensor", swap)
    return [part, beside, near, far, lax.ppermute(near, "tensor", swap), lax.ppermute(far, "tensor", swap)]


def shards(final_input, norm_gain, value_weight, out_weight, cluster, priority):
    rows, width = final_input.shape
    splits = lax.axis_size("tensor")
    owners = lax.axis_size("dp")
    clusters = splits * owners
    depth = blocks(width) + 2
    flat, message, half = pack(
        cluster.reshape(1, rows),
        priority.reshape(1, rows),
        final_input,
        value_weight,
        clusters,
        depth,
        owners * rows,
    )
    projects = spread_halves(value_weight, half, splits, owners)
    got = lax.all_to_all(message.reshape(clusters, depth // 2, 2, LANES), AXES, 0, 0, tiled=True)
    got = got.reshape(clusters * depth, LANES)
    out_weight, _, _ = lax.optimization_barrier((out_weight, flat, projects[2]))
    folded, folded_half = fold(out_weight)
    weights = spread_halves(folded, folded_half, splits, owners)
    best = owner_best(norm_gain.reshape(blocks(width), LANES), got, projects, weights, clusters)
    returned = lax.all_to_all(best, AXES, 0, 0, tiled=True)
    return pick(flat, returned).reshape(rows)


def solution(mesh):
    in_specs = (P("dp", None), P(), P(None, "tensor"), P("tensor", None), P("dp", None), P("dp"))
    return jax.shard_map(shards, mesh=mesh, in_specs=in_specs, out_specs=P("dp"), check_vma=False)
```

time: 123 us -> 119 us (0.967)
  waiting for transfers between devices: 51.6 us -> 34.4 us
  starting transfers between devices: 22.6 us -> 33.2 us
  other arithmetic: 6.91 us -> 0 us
  Pallas kernels: 18.3 us -> 24.4 us
  local copies, waits for them, and re-layouts: 2.92 us -> 4.61 us
  blocking collectives: 20.5 us -> 21.9 us
    ppermute x3 -> x10, starting transfers between devices: 6.91 us -> 18.8 us  [the longest x2 6.06 us: spread_halves(): near = lax.ppermute(half, AXES, ring_pairs(splits, owners))]
    pallas_call x1 -> x2, Pallas kernels: 7.73 us -> 16.9 us  [the longest x1 11.5 us: owner_best(): pl.pallas_call(owner_kernel, in_specs=[vmem] + [hbm] * (1 + len(projects)...]
    ppermute x3 -> x10, waiting for transfers between devices: 43.2 us -> 34.4 us  [the longest x2 18.1 us: spread_halves(): near = lax.ppermute(half, AXES, ring_pairs(splits, owners))]
    all_to_all x1, waiting for transfers between devices: 8.39 us -> 0.01 us  [shards(): lax.all_to_all(message.reshape(clusters, depth // 2, 2, LANES), AXES, 0,...]
    reduce_sum x1 -> x0, other arithmetic: 6.91 us -> none  [shards(): jnp.sum(out_weight.reshape(kv_local, group, HEAD_DIM, width).astype(F32),...]
    pallas_call x1, Pallas kernels: 8.7 us -> 5.62 us  [pack(): pl.pallas_call(functools.partial(pack_kernel, sentinel), in_specs=[vmem,...]
    unnamed x6 -> x22, local copies, waits for them, and re-layouts: 2.92 us -> 4.61 us
    all_to_all x1, blocking collectives: 20.5 us -> 21.9 us  [shards(): returned = lax.all_to_all(best, AXES, 0, 0, tiled=True)]
  transfers between devices with their start and end apart: 4 -> 11, of which waited for: 3 -> 3; matrix products, arithmetic and copies ran while one was open for 6% -> 0% of each run, Pallas kernels for 0% -> 5%
where the time goes in v3:
time: 119 us
  waiting for transfers between devices  34.4 us (29%)
  starting transfers between devices  33.2 us (28%)
  Pallas kernels  24.4 us (21%)
  blocking collectives  21.9 us (18%)
  local copies, waits for them, and re-layouts  4.61 us (4%)
    all_to_all x1, blocking collectives, shards(): returned = lax.all_to_all(best, AXES, 0, 0, tiled=True)  21.9 us
    ppermute x2, waiting for transfers between devices, spread_halves(): near = lax.ppermute(half, AXES, ring_pairs(splits, owners))  18.1 us
    ppermute x2, waiting for transfers between devices, spread_halves(): far = lax.ppermute(near, AXES, column_pairs(splits, owners))  15.3 us
    all_to_all x1, starting transfers between devices, shards(): lax.all_to_all(message.reshape(clusters, depth // 2, 2, LANES), AXES, 0,...  14.4 us
    pallas_call x1, Pallas kernels, owner_best(): pl.pallas_call(owner_kernel, in_specs=[vmem] + [hbm] * (1 + len(projects)...  11.5 us
    ppermute x2, starting transfers between devices, spread_halves(): near = lax.ppermute(half, AXES, ring_pairs(splits, owners))  6.06 us
    ppermute x2, starting transfers between devices, spread_halves(): lax.ppermute(far, 'tensor', swap)  5.85 us
    pallas_call x1, Pallas kernels, pack(): pl.pallas_call(functools.partial(pack_kernel, sentinel), in_specs=[vmem,...  5.62 us
  transfers between devices with their start and end apart: 11, of which 3 were waited for; matrix products, arithmetic and copies ran while one was open for 0% of the time, Pallas kernels for 5%

profile of v3, /device:TPU:1, one launch (start us, length us, event | category | flops | bytes accessed | tf_op | source)
XLA Modules:
  0.0 118.6 jit_solution(3465880727025252787)
XLA Ops:
  0.0 5.6 %pack.1 = (s32[8,512]{1,0:T(8,128)}, bf16[8704,128]{1,0:T(8,128)(2,1)}, bf16[2048,256]{1,0:T(8,128)(2,1)}) custom-call(s32[1,512]{1,0:T(1,128)} %bitcast.12, s32[1,512]{1,0:T(1,128)} %bitcast.13, bf16[512,4096]{1,0:T(8,128)(2,1)} %x_hbm.1, bf16[4096,256]{1,0:T(8,128)(2,1)} %v0.1), custom_call_target="tpu_custom_call" | custom-call | flops 1073741824 | bytes 6291456 | tf_op jit(solution)/shard_map/pack/pallas_call | solution.py:105
  5.6 3.4 %collective-permute-start.1 = (bf16[2048,256]{1,0:T(8,128)(2,1)}, bf16[2048,256]{1,0:T(8,128)(2,1)S(1)}, u32[]{:S(2)}, u32[]{:S(2)}) collective-permute-start(bf16[2048,256]{1,0:T(8,128)(2,1)} %get-tuple-element.13), channel_id=1, source_target_pairs={{0,2},{1,7},{2,4},{3,1},{4,6},{5,3},{6,0},{7,5},{8,10},{9,15},{10,... | collective-permute-start | bytes 3145736 | tf_op jit(solution)/shard_map/ppermute | solution.py:392
  9.0 14.4 %all-to-all-start = ((bf16[256,17,2,128]{3,2,1,0:T(2,128)(2,1)}), bf16[256,17,2,128]{3,2,1,0:T(2,128)(2,1)}, u32[]{:S(2)}, u32[]{:S(2)}) async-start(bf16[256,17,2,128]{3,2,1,0:T(2,128)(2,1)} %bitcast.3), calls=%async_computation | async-start | bytes 4456448 | tf_op jit(solution)/shard_map/all_to_all | solution.py:414
  23.4 0.0 collective-permute-done.1.v2
  23.5 0.0 copy-start.2
  23.5 1.0 copy-done.2
  24.4 0.0 copy-start
  24.4 0.0 copy-start.3
  24.4 5.4 %fold.1 = (bf16[256,4096]{1,0:T(8,128)(2,1)}, bf16[128,4096]{1,0:T(8,128)(2,1)}) custom-call(bf16[1024,4096]{1,0:T(8,128)(2,1)} %weight_hbm), custom_call_target="tpu_custom_call" | custom-call | flops 399999991808 | bytes 10485760 | tf_op jit(solution)/shard_map/fold/pallas_call | solution.py:165
  29.9 2.7 %collective-permute-start.6 = (bf16[128,4096]{1,0:T(8,128)(2,1)}, bf16[128,4096]{1,0:T(8,128)(2,1)S(1)}, u32[]{:S(2)}, u32[]{:S(2)}) collective-permute-start(bf16[128,4096]{1,0:T(8,128)(2,1)} %get-tuple-element.16), channel_id=1, source_target_pairs={{0,2},{1,7},{2,4},{3,1},{4,6},{5,3},{6,0},{7,5},{8,10},{9,15},{10,... | collective-permute-start | bytes 3145736 | tf_op jit(solution)/shard_map/ppermute | solution.py:392
  32.6 0.0 copy-done
  32.6 0.0 collective-permute-start
  32.6 0.0 copy-done.3
  32.6 2.6 %collective-permute-start.2 = (bf16[2048,256]{1,0:T(8,128)(2,1)S(1)}, bf16[2048,256]{1,0:T(8,128)(2,1)S(1)}, u32[]{:S(2)}, u32[]{:S(2)}) collective-permute-start(bf16[2048,256]{1,0:T(8,128)(2,1)S(1)} %copy-done.3), channel_id=1, source_target_pairs={{0,8},{1,25},{2,10},{3,27},{4,12},{5,29},{6,14},{7,31},{8,16},{9,1... | collective-permute-start | bytes 3145736 | tf_op jit(solution)/shard_map/ppermute | solution.py:393
  35.1 18.1 %collective-permute-done.6.w2 = bf16[128,4096]{1,0:T(8,128)(2,1)S(1)} collective-permute-done((bf16[128,4096]{1,0:T(8,128)(2,1)}, bf16[128,4096]{1,0:T(8,128)(2,1)S(1)}, u32[]{:S(2)}, u32[]{:S(2)}) %collective-permute-start.6) | collective-permute-done | bytes 1048608 | tf_op jit(solution)/shard_map/ppermute | solution.py:392
  53.3 0.0 copy-start.4
  53.3 2.8 %collective-permute-start.7 = (bf16[128,4096]{1,0:T(8,128)(2,1)S(1)}, bf16[128,4096]{1,0:T(8,128)(2,1)S(1)}, u32[]{:S(2)}, u32[]{:S(2)}) collective-permute-start(bf16[128,4096]{1,0:T(8,128)(2,1)S(1)} %collective-permute-done.6.w2), channel_id=1, source_target_pairs={{0,8},{1,25},{2,10},{3,27},{4,12},{5,29},{6,14},{7,31},{8,16},{9,1... | collective-permute-start | bytes 3145736 | tf_op jit(solution)/shard_map/ppermute | solution.py:393
  56.1 1.4 %collective-permute-start.5 = (bf16[256,4096]{1,0:T(8,128)(2,1)}, bf16[256,4096]{1,0:T(8,128)(2,1)}, u32[]{:S(2)}, u32[]{:S(2)}) collective-permute-start(bf16[256,4096]{1,0:T(8,128)(2,1)} %get-tuple-element.15.w0), channel_id=1, source_target_pairs={{0,1},{1,0},{2,3},{3,2},{4,5},{5,4},{6,7},{7,6},{8,9},{9,8},{10,11... | collective-permute-start | bytes 6291464 | tf_op jit(solution)/shard_map/ppermute | solution.py:394
  57.5 0.1 collective-permute-start.3
  57.5 0.0 collective-permute-done.2.v2y
  57.5 0.0 copy-start.5
  57.6 1.1 collective-permute-start.4
  58.6 0.0 collective-permute-done.v1
  58.6 0.0 copy-start.1
  58.6 1.4 %copy-done.1 = bf16[4096,256]{1,0:T(8,128)(2,1)} copy-done((bf16[4096,256]{1,0:T(8,128)(2,1)}, bf16[4096,256]{1,0:T(8,128)(2,1)S(1)}, u32[]{:S(2)}) %copy-start.1) | copy-done | bytes 2097176
  60.0 0.0 collective-permute-start.8
  60.0 15.3 %collective-permute-done.7.w2y = bf16[128,4096]{1,0:T(8,128)(2,1)S(1)} collective-permute-done((bf16[128,4096]{1,0:T(8,128)(2,1)S(1)}, bf16[128,4096]{1,0:T(8,128)(2,1)S(1)}, u32[]{:S(2)}, u32[]{:S(2)}) %collective-permute-start.7) | collective-permute-done | bytes 1048608 | tf_op jit(solution)/shard_map/ppermute | solution.py:393
  75.4 0.0 copy-start.6
  75.4 4.8 %collective-permute-start.9 = (bf16[128,4096]{1,0:T(8,128)(2,1)S(1)}, bf16[128,4096]{1,0:T(8,128)(2,1)S(1)}, u32[]{:S(2)}, u32[]{:S(2)}) collective-permute-start(bf16[128,4096]{1,0:T(8,128)(2,1)S(1)} %collective-permute-done.7.w2y), channel_id=1, source_target_pairs={{0,1},{1,0},{2,3},{3,2},{4,5},{5,4},{6,7},{7,6},{8,9},{9,8},{10,11... | collective-permute-start | bytes 3145736 | tf_op jit(solution)/shard_map/ppermute | solution.py:395
  80.2 0.0 collective-permute-done.3.v3
  80.2 0.0 copy-done.4
  80.2 0.0 copy-start.7
  80.2 0.0 collective-permute-done.4.v3y
  80.2 0.0 copy-start.8
  80.2 0.0 collective-permute-done.8.w3
  80.2 0.0 copy-done.5
  80.2 0.0 copy-start.9
  80.2 0.0 collective-permute-done.5.w1
  80.2 0.0 copy-done.6
  80.3 0.9 copy-done.7
  81.2 0.3 copy-done.8
  81.5 1.0 collective-permute-done.9.w3y
  82.5 0.0 all-to-all-done
  82.5 0.0 copy-done.9
  82.5 1.0 copy-done.10
  83.4 11.5 %owner_best.1 = f32[256,128]{1,0:T(8,128)} custom-call(bf16[32,128]{1,0:T(8,128)(2,1)} %bitcast.14, bf16[8704,128]{1,0:T(8,128)(2,1)} %bitcast.4.got_hbm, bf16[4096,256]{1,0:T(8,128)(2,1)} %v0.1, bf16[4096,256]{1,0:T(8,128)(2,1)} %copy-done.1, bf16[2048,256]{1,0:T(8,128)(2,1)} %copy-done.2, bf16[2048,256]{1,0:T(8,128)(2,1)} %copy-done.5, ...), custom_call_target="tpu_custom_call" | custom-call | flops 6442450944 | bytes 20971520 | tf_op jit(solution)/shard_map/owner_best/pallas_call | solution.py:316
  94.9 21.9 %all_to_all.16 = f32[256,1,128]{2,1,0:T(1,128)} all-to-all(f32[256,1,128]{2,1,0:T(1,128)} %bitcast.11), channel_id=1, replica_groups=mesh['dp'=64,'tensor'=4] {'dp','tensor'}, dimensions={0} | all-to-all | bytes 262144 | tf_op jit(solution)/shard_map/all_to_all | solution.py:420
  116.8 1.9 %pick.1 = f32[1,512]{1,0:T(1,128)} custom-call(s32[8,512]{1,0:T(8,128)} %get-tuple-element.11.flat_ref, f32[256,128]{1,0:T(8,128)} %bitcast.10), custom_call_target="tpu_custom_call" | custom-call | tf_op jit(solution)/shard_map/pick/pallas_call | solution.py:357
  (1 shorter events, 0.0 us)
Async XLA Ops:
  5.6 17.8 %collective-permute-start.1 = (bf16[2048,256]{1,0:T(8,128)(2,1)}, bf16[2048,256]{1,0:T(8,128)(2,1)S(1)}, u32[]{:S(2)}, u32[]{:S(2)}) collective-permute-start(bf16[2048,256]{1,0:T(8,128)(2,1)} %get-tuple-element.13), channel_id=1, source_target_pairs={{0,2},{1,7},{2,4},{3,1},{4,6},{5,3},{6,0},{7,5},{8,10},{9,15},{10,... | collective-permute-start | bytes 3145736 | tf_op jit(solution)/shard_map/ppermute | solution.py:392
  9.0 73.5 %all-to-all-start = ((bf16[256,17,2,128]{3,2,1,0:T(2,128)(2,1)}), bf16[256,17,2,128]{3,2,1,0:T(2,128)(2,1)}, u32[]{:S(2)}, u32[]{:S(2)}) async-start(bf16[256,17,2,128]{3,2,1,0:T(2,128)(2,1)} %bitcast.3), calls=%async_computation | async-start | bytes 4456448 | tf_op jit(solution)/shard_map/all_to_all | solution.py:414
  23.5 1.0 copy-start.2
  24.4 8.1 %copy-start = (bf16[4096,256]{1,0:T(8,128)(2,1)S(1)}, bf16[4096,256]{1,0:T(8,128)(2,1)}, u32[]{:S(2)}) copy-start(bf16[4096,256]{1,0:T(8,128)(2,1)} %v0.1) | copy-start | bytes 6291460
  24.4 8.1 %copy-start.3 = (bf16[2048,256]{1,0:T(8,128)(2,1)S(1)}, bf16[2048,256]{1,0:T(8,128)(2,1)}, u32[]{:S(2)}) copy-start(bf16[2048,256]{1,0:T(8,128)(2,1)} %copy-done.2) | copy-start | bytes 3145732
  29.9 23.4 %collective-permute-start.6 = (bf16[128,4096]{1,0:T(8,128)(2,1)}, bf16[128,4096]{1,0:T(8,128)(2,1)S(1)}, u32[]{:S(2)}, u32[]{:S(2)}) collective-permute-start(bf16[128,4096]{1,0:T(8,128)(2,1)} %get-tuple-element.16), channel_id=1, source_target_pairs={{0,2},{1,7},{2,4},{3,1},{4,6},{5,3},{6,0},{7,5},{8,10},{9,15},{10,... | collective-permute-start | bytes 3145736 | tf_op jit(solution)/shard_map/ppermute | solution.py:392
  32.6 26.0 %collective-permute-start = (bf16[4096,256]{1,0:T(8,128)(2,1)S(1)}, bf16[4096,256]{1,0:T(8,128)(2,1)S(1)}, u32[]{:S(2)}, u32[]{:S(2)}) collective-permute-start(bf16[4096,256]{1,0:T(8,128)(2,1)S(1)} %copy-done), channel_id=1, source_target_pairs={{0,1},{1,0},{2,3},{3,2},{4,5},{5,4},{6,7},{7,6},{8,9},{9,8},{10,11... | collective-permute-start | bytes 6291464 | tf_op jit(solution)/shard_map/ppermute | solution.py:394
  32.6 25.0 %collective-permute-start.2 = (bf16[2048,256]{1,0:T(8,128)(2,1)S(1)}, bf16[2048,256]{1,0:T(8,128)(2,1)S(1)}, u32[]{:S(2)}, u32[]{:S(2)}) collective-permute-start(bf16[2048,256]{1,0:T(8,128)(2,1)S(1)} %copy-done.3), channel_id=1, source_target_pairs={{0,8},{1,25},{2,10},{3,27},{4,12},{5,29},{6,14},{7,31},{8,16},{9,1... | collective-permute-start | bytes 3145736 | tf_op jit(solution)/shard_map/ppermute | solution.py:393
  53.3 26.9 %copy-start.4 = (bf16[128,4096]{1,0:T(8,128)(2,1)}, bf16[128,4096]{1,0:T(8,128)(2,1)S(1)}, u32[]{:S(2)}) copy-start(bf16[128,4096]{1,0:T(8,128)(2,1)S(1)} %collective-permute-done.6.w2) | copy-start | bytes 3145732
  53.3 22.1 %collective-permute-start.7 = (bf16[128,4096]{1,0:T(8,128)(2,1)S(1)}, bf16[128,4096]{1,0:T(8,128)(2,1)S(1)}, u32[]{:S(2)}, u32[]{:S(2)}) collective-permute-start(bf16[128,4096]{1,0:T(8,128)(2,1)S(1)} %collective-permute-done.6.w2), channel_id=1, source_target_pairs={{0,8},{1,25},{2,10},{3,27},{4,12},{5,29},{6,14},{7,31},{8,16},{9,1... | collective-permute-start | bytes 3145736 | tf_op jit(solution)/shard_map/ppermute | solution.py:393
  56.1 24.2 %collective-permute-start.5 = (bf16[256,4096]{1,0:T(8,128)(2,1)}, bf16[256,4096]{1,0:T(8,128)(2,1)}, u32[]{:S(2)}, u32[]{:S(2)}) collective-permute-start(bf16[256,4096]{1,0:T(8,128)(2,1)} %get-tuple-element.15.w0), channel_id=1, source_target_pairs={{0,1},{1,0},{2,3},{3,2},{4,5},{5,4},{6,7},{7,6},{8,9},{9,8},{10,11... | collective-permute-start | bytes 6291464 | tf_op jit(solution)/shard_map/ppermute | solution.py:394
  57.5 22.7 %collective-permute-start.3 = (bf16[2048,256]{1,0:T(8,128)(2,1)S(1)}, bf16[2048,256]{1,0:T(8,128)(2,1)S(1)}, u32[]{:S(2)}, u32[]{:S(2)}) collective-permute-start(bf16[2048,256]{1,0:T(8,128)(2,1)S(1)} %copy-done.3), channel_id=1, source_target_pairs={{0,1},{1,0},{2,3},{3,2},{4,5},{5,4},{6,7},{7,6},{8,9},{9,8},{10,11... | collective-permute-start | bytes 3145736 | tf_op jit(solution)/shard_map/ppermute | solution.py:395
  57.5 22.7 %copy-start.5 = (bf16[2048,256]{1,0:T(8,128)(2,1)}, bf16[2048,256]{1,0:T(8,128)(2,1)S(1)}, u32[]{:S(2)}) copy-start(bf16[2048,256]{1,0:T(8,128)(2,1)S(1)} %collective-permute-done.2.v2y) | copy-start | bytes 3145732
  57.6 22.6 %collective-permute-start.4 = (bf16[2048,256]{1,0:T(8,128)(2,1)S(1)}, bf16[2048,256]{1,0:T(8,128)(2,1)S(1)}, u32[]{:S(2)}, u32[]{:S(2)}) collective-permute-start(bf16[2048,256]{1,0:T(8,128)(2,1)S(1)} %collective-permute-done.2.v2y), channel_id=1, source_target_pairs={{0,1},{1,0},{2,3},{3,2},{4,5},{5,4},{6,7},{7,6},{8,9},{9,8},{10,11... | collective-permute-start | bytes 3145736 | tf_op jit(solution)/shard_map/ppermute | solution.py:395
  58.6 1.4 %copy-start.1 = (bf16[4096,256]{1,0:T(8,128)(2,1)}, bf16[4096,256]{1,0:T(8,128)(2,1)S(1)}, u32[]{:S(2)}) copy-start(bf16[4096,256]{1,0:T(8,128)(2,1)S(1)} %collective-permute-done.v1) | copy-start | bytes 6291460
  60.0 20.2 %collective-permute-start.8 = (bf16[128,4096]{1,0:T(8,128)(2,1)S(1)}, bf16[128,4096]{1,0:T(8,128)(2,1)S(1)}, u32[]{:S(2)}, u32[]{:S(2)}) collective-permute-start(bf16[128,4096]{1,0:T(8,128)(2,1)S(1)} %collective-permute-done.6.w2), channel_id=1, source_target_pairs={{0,1},{1,0},{2,3},{3,2},{4,5},{5,4},{6,7},{7,6},{8,9},{9,8},{10,11... | collective-permute-start | bytes 3145736 | tf_op jit(solution)/shard_map/ppermute | solution.py:395
  75.4 4.9 %copy-start.6 = (bf16[128,4096]{1,0:T(8,128)(2,1)}, bf16[128,4096]{1,0:T(8,128)(2,1)S(1)}, u32[]{:S(2)}) copy-start(bf16[128,4096]{1,0:T(8,128)(2,1)S(1)} %collective-permute-done.7.w2y) | copy-start | bytes 3145732
  75.4 7.1 %collective-permute-start.9 = (bf16[128,4096]{1,0:T(8,128)(2,1)S(1)}, bf16[128,4096]{1,0:T(8,128)(2,1)S(1)}, u32[]{:S(2)}, u32[]{:S(2)}) collective-permute-start(bf16[128,4096]{1,0:T(8,128)(2,1)S(1)} %collective-permute-done.7.w2y), channel_id=1, source_target_pairs={{0,1},{1,0},{2,3},{3,2},{4,5},{5,4},{6,7},{7,6},{8,9},{9,8},{10,11... | collective-permute-start | bytes 3145736 | tf_op jit(solution)/shard_map/ppermute | solution.py:395
  80.2 1.0 copy-start.7
  80.2 1.3 %copy-start.8 = (bf16[2048,256]{1,0:T(8,128)(2,1)}, bf16[2048,256]{1,0:T(8,128)(2,1)S(1)}, u32[]{:S(2)}) copy-start(bf16[2048,256]{1,0:T(8,128)(2,1)S(1)} %collective-permute-done.4.v3y) | copy-start | bytes 3145732
  80.2 2.2 %copy-start.9 = (bf16[128,4096]{1,0:T(8,128)(2,1)}, bf16[128,4096]{1,0:T(8,128)(2,1)S(1)}, u32[]{:S(2)}) copy-start(bf16[128,4096]{1,0:T(8,128)(2,1)S(1)} %collective-permute-done.8.w3) | copy-start | bytes 3145732
  82.5 1.0 copy-start.10

commit v4 on v3

--- a/solution.py
+++ b/solution.py
@@ -21,7 +21,8 @@
 OWNER_PARTS = 4
 PROJECT_PARTS = 4
 AHEAD = 3
-FOLD_PARTS = 8
+FOLD_PARTS = 4
+FOLD_LIMIT = 12
 RANK_BASE = 128
 
 
@@ -125,72 +126,66 @@
     )(cluster, priority, x, project)
 
 
-def fold_kernel(weight_hbm, out_hbm, half_hbm, weight_ref, out_ref, in_sems, out_sems, half_sem):
-    group = HEADS // KV_HEADS
-    kv_part, width = out_ref.shape
+def fold_kernel(near, weight_hbm, out_hbm, weight_ref, out_ref, in_sems, out_sems):
+    group, width = HEADS // KV_HEADS, out_ref.shape[1]
+    height = weight_ref.shape[0]
+    chosen_half = row_parity() if near else 1 - row_parity()
+    begin = pl.multiple_of(chosen_half * height, height)
     part = width // FOLD_PARTS
     in_copies = []
     for j in range(FOLD_PARTS):
         cols = pl.ds(j * part, part)
-        copy = pltpu.make_async_copy(weight_hbm.at[:, cols], weight_ref.at[:, cols], in_sems.at[j])
+        copy = pltpu.make_async_copy(
+            weight_hbm.at[pl.ds(begin, height), cols], weight_ref.at[:, cols], in_sems.at[j]
+        )
         copy.start()
         in_copies.append(copy)
     out_copies = []
     for j in range(FOLD_PARTS):
         in_copies[j].wait()
         cols = slice(j * part, (j + 1) * part)
-        for kv in range(kv_part // HEAD_DIM):
-            total = 0.0
-            for g in range(group):
-                start = (kv * group + g) * HEAD_DIM
-                total = total + weight_ref[start : start + HEAD_DIM, cols].astype(F32)
-            out_ref[kv * HEAD_DIM : (kv + 1) * HEAD_DIM, cols] = total.astype(BF16)
+        total = 0.0
+        for g in range(group):
+            total = total + weight_ref[g * HEAD_DIM : (g + 1) * HEAD_DIM, cols].astype(F32)
+        out_ref[:, cols] = total.astype(BF16)
         span = pl.ds(j * part, part)
         copy = pltpu.make_async_copy(out_ref.at[:, span], out_hbm.at[:, span], out_sems.at[j])
         copy.start()
         out_copies.append(copy)
-    half = half_hbm.shape[0]
-    start = pl.multiple_of(row_parity() * half, half)
-    copy = pltpu.make_async_copy(out_ref.at[pl.ds(start, half), :], half_hbm, half_sem)
-    copy.start()
-    out_copies.append(copy)
     for copy in out_copies:
         copy.wait()
 
 
-def fold(out_weight):
+def fold(out_weight, near):
     height, width = out_weight.shape
-    kv_part = height * KV_HEADS // HEADS
     hbm = pl.BlockSpec(memory_space=pl.ANY)
     return pl.pallas_call(
-        fold_kernel,
+        functools.partial(fold_kernel, near),
         in_specs=[hbm],
-        out_specs=[hbm, hbm],
-        out_shape=[
-            jax.ShapeDtypeStruct((kv_part, width), BF16),
-            jax.ShapeDtypeStruct((kv_part // 2, width), BF16),
-        ],
+        out_specs=hbm,
+        out_shape=jax.ShapeDtypeStruct((HEAD_DIM, width), BF16),
         scratch_shapes=[
-            pltpu.VMEM(out_weight.shape, BF16),
-            pltpu.VMEM((kv_part, width), BF16),
+            pltpu.VMEM((height // 2, width), BF16),
+            pltpu.VMEM((HEAD_DIM, width), BF16),
             pltpu.SemaphoreType.DMA((FOLD_PARTS,)),
             pltpu.SemaphoreType.DMA((FOLD_PARTS,)),
-            pltpu.SemaphoreType.DMA,
         ],
-        compiler_params=pltpu.CompilerParams(vmem_limit_bytes=58 * MIB),
-        cost_estimate=pl.CostEstimate(flops=4 * 10**11, bytes_accessed=10 * MIB, transcendentals=0),
-        name="fold",
-    )(out_weight)
+        compiler_params=pltpu.CompilerParams(vmem_limit_bytes=FOLD_LIMIT * MIB),
+        cost_estimate=pl.CostEstimate(
+            flops=4 * 10**11 if near else 4 * MIB, bytes_accessed=5 * MIB, transcendentals=0
+        ),
+        name="fold_near" if near else "fold_far",
+    )(pltpu.with_memory_space_constraint(out_weight, pltpu.MemorySpace.HBM))
 
 
 def owner_kernel(
-    gain_ref, got_hbm, v0, v1, v2, v2y, v3, v3y, w0, w1, w2, w2y, w3, w3y, out_ref,
+    gain_ref, got_hbm, v0, v1, v2, v2y, v3, v3y, w0, w0y, w1, w1y, w2, w2y, w3, w3y, out_ref,
     got_ref, wide_ref, x_ref, gained_ref, project_ref, weight_ref, high, low, gram_ref, cross_ref, product_ref,
     got_sems, project_sems, weight_sems,
 ):
     clusters, width = high.shape
     depth = got_ref.shape[0] // clusters
-    kv_part = w0.shape[0]
+    kv_part = v0.shape[1]
     share = got_ref.shape[0] // ROW_PARTS
     got_copies = []
     for q in range(ROW_PARTS):
@@ -225,10 +220,9 @@
     for j in range(OWNER_PARTS):
         cols = pl.ds(j * part, part)
         group = []
-        for i, (source, n, shift) in enumerate(
-            ((w0, 0, 0), (w1, 1, 0), (w2, 2, near), (w2y, 2, far), (w3, 3, near), (w3y, 3, far))
-        ):
-            span = pl.ds(pl.multiple_of(n * kv_part + shift, rows), source.shape[0])
+        for i, source in enumerate((w0, w0y, w1, w1y, w2, w2y, w3, w3y)):
+            shift = near if i % 2 == 0 else far
+            span = pl.ds(pl.multiple_of(i // 2 * kv_part + shift, rows), rows)
             group.append(
                 pltpu.make_async_copy(source.at[:, cols], weight_ref.at[span, cols], weight_sems.at[j, i])
             )
@@ -309,7 +303,7 @@
 
 
 def owner_best(gain, got, projects, weights, clusters):
-    kv_part, width = weights[0].shape
+    width, kv_part = projects[0].shape
     height = kv_part * SLOTS
     hbm = pl.BlockSpec(memory_space=pl.ANY)
     vmem = pl.BlockSpec(memory_space=pltpu.VMEM)
@@ -387,12 +381,11 @@
     return pairs
 
 
-def spread_halves(part, half, splits, owners):
+def cross(near, splits, owners):
     swap = [(t, t ^ 1) for t in range(splits)]
-    near = lax.ppermute(half, AXES, ring_pairs(splits, owners))
-    far = lax.ppermute(near, AXES, column_pairs(splits, owners))
-    beside = lax.ppermute(part, "tensor", swap)
-    return [part, beside, near, far, lax.ppermute(near, "tensor", swap), lax.ppermute(far, "tensor", swap)]
+    across = lax.ppermute(near, AXES, ring_pairs(splits, owners))
+    along = lax.ppermute(across, AXES, column_pairs(splits, owners))
+    return [across, along, lax.ppermute(across, "tensor", swap), lax.ppermute(along, "tensor", swap)]
 
 
 def shards(final_input, norm_gain, value_weight, out_weight, cluster, priority):
@@ -410,12 +403,16 @@
         depth,
         owners * rows,
     )
-    projects = spread_halves(value_weight, half, splits, owners)
+    swap = [(t, t ^ 1) for t in range(splits)]
+    projects = [value_weight, lax.ppermute(value_weight, "tensor", swap), *cross(half, splits, owners)]
     got = lax.all_to_all(message.reshape(clusters, depth // 2, 2, LANES), AXES, 0, 0, tiled=True)
     got = got.reshape(clusters * depth, LANES)
     out_weight, _, _ = lax.optimization_barrier((out_weight, flat, projects[2]))
-    folded, folded_half = fold(out_weight)
-    weights = spread_halves(folded, folded_half, splits, owners)
+    near = fold(out_weight, True)
+    out_weight, near = lax.optimization_barrier((out_weight, near))
+    far = fold(out_weight, False)
+    beside = [lax.ppermute(w, "tensor", swap) for w in (near, far)]
+    weights = [near, far, *beside, *cross(near, splits, owners)]
     best = owner_best(norm_gain.reshape(blocks(width), LANES), got, projects, weights, clusters)
     returned = lax.all_to_all(best, AXES, 0, 0, tiled=True)
     return pick(flat, returned).reshape(rows)

time: 119 us -> 116 us (0.975)
  local copies, waits for them, and re-layouts: 4.61 us -> 2.54 us
  waiting for transfers between devices: 34.4 us -> 32.4 us
    ppermute x10 -> x11, waiting for transfers between devices: 34.4 us -> 32.3 us  [the longest x2 17.6 us: cross(): along = lax.ppermute(across, AXES, column_pairs(splits, owners))]
    unnamed x22 -> x24, local copies, waits for them, and re-layouts: 4.61 us -> 2.54 us
    ppermute x10 -> x11, starting transfers between devices: 18.8 us -> 19.8 us  [the longest x2 6.14 us: cross(): lax.ppermute(along, 'tensor', swap)]
    pallas_call x1 -> x2, Pallas kernels: 5.43 us -> 5.29 us  [fold(): pl.pallas_call(functools.partial(fold_kernel, near), in_specs=[hbm], out_...]
  transfers between devices with their start and end apart: 11 -> 12, of which waited for: 3 -> 3; matrix products, arithmetic and copies ran while one was open for 0% -> 0% of each run, Pallas kernels for 5% -> 5%
where the time goes in v4:
time: 116 us
  starting transfers between devices  34.3 us (30%)
  waiting for transfers between devices  32.4 us (28%)
  Pallas kernels  24.3 us (21%)
  blocking collectives  22.3 us (19%)
  local copies, waits for them, and re-layouts  2.54 us (2%)
    all_to_all x1, blocking collectives, shards(): returned = lax.all_to_all(best, AXES, 0, 0, tiled=True)  22.3 us
    ppermute x2, waiting for transfers between devices, cross(): along = lax.ppermute(across, AXES, column_pairs(splits, owners))  17.6 us
    ppermute x2, waiting for transfers between devices, cross(): across = lax.ppermute(near, AXES, ring_pairs(splits, owners))  14.7 us
    all_to_all x1, starting transfers between devices, shards(): lax.all_to_all(message.reshape(clusters, depth // 2, 2, LANES), AXES, 0,...  14.5 us
    pallas_call x1, Pallas kernels, owner_best(): pl.pallas_call(owner_kernel, in_specs=[vmem] + [hbm] * (1 + len(projects)...  11.6 us
    ppermute x2, starting transfers between devices, cross(): lax.ppermute(along, 'tensor', swap)  6.14 us
    ppermute x2, starting transfers between devices, cross(): across = lax.ppermute(near, AXES, ring_pairs(splits, owners))  6.06 us
    ppermute x2, starting transfers between devices, cross(): along = lax.ppermute(across, AXES, column_pairs(splits, owners))  5.87 us
  transfers between devices with their start and end apart: 12, of which 3 were waited for; matrix products, arithmetic and copies ran while one was open for 0% of the time, Pallas kernels for 5%

profile of v4, /device:TPU:1, one launch (start us, length us, event | category | flops | bytes accessed | tf_op | source)
XLA Modules:
  0.0 116.0 jit_solution(10741761782840061782)
XLA Ops:
  0.0 5.6 %pack.1 = (s32[8,512]{1,0:T(8,128)}, bf16[8704,128]{1,0:T(8,128)(2,1)}, bf16[2048,256]{1,0:T(8,128)(2,1)}) custom-call(s32[1,512]{1,0:T(1,128)} %bitcast.12, s32[1,512]{1,0:T(1,128)} %bitcast.13, bf16[512,4096]{1,0:T(8,128)(2,1)} %x_hbm.1, bf16[4096,256]{1,0:T(8,128)(2,1)} %v0.1), custom_call_target="tpu_custom_call" | custom-call | flops 1073741824 | bytes 6291456 | tf_op jit(solution)/shard_map/pack/pallas_call | solution.py:106
  5.6 3.4 %collective-permute-start.1 = (bf16[2048,256]{1,0:T(8,128)(2,1)}, bf16[2048,256]{1,0:T(8,128)(2,1)S(1)}, u32[]{:S(2)}, u32[]{:S(2)}) collective-permute-start(bf16[2048,256]{1,0:T(8,128)(2,1)} %get-tuple-element.13), channel_id=1, source_target_pairs={{0,2},{1,7},{2,4},{3,1},{4,6},{5,3},{6,0},{7,5},{8,10},{9,15},{10,... | collective-permute-start | bytes 3145736 | tf_op jit(solution)/shard_map/ppermute | solution.py:386
  9.0 0.0 collective-permute-start
  9.0 14.5 %all-to-all-start = ((bf16[256,17,2,128]{3,2,1,0:T(2,128)(2,1)}), bf16[256,17,2,128]{3,2,1,0:T(2,128)(2,1)}, u32[]{:S(2)}, u32[]{:S(2)}) async-start(bf16[256,17,2,128]{3,2,1,0:T(2,128)(2,1)} %bitcast.3), calls=%async_computation | async-start | bytes 4456448 | tf_op jit(solution)/shard_map/all_to_all | solution.py:408
  23.5 0.0 collective-permute-done.1.v2
  23.5 0.0 copy-start.2
  23.5 2.8 %fold_near.1.w0 = bf16[128,4096]{1,0:T(8,128)(2,1)S(1)} custom-call(bf16[1024,4096]{1,0:T(8,128)(2,1)} %weight_hbm.1), custom_call_target="tpu_custom_call" | custom-call | flops 399999991808 | bytes 5242880 | tf_op jit(solution)/shard_map/fold_near/pallas_call | solution.py:162
  26.3 0.0 copy-done.2
  26.4 0.0 copy-start.1
  26.4 2.7 %collective-permute-start.7 = (bf16[128,4096]{1,0:T(8,128)(2,1)S(1)}, bf16[128,4096]{1,0:T(8,128)(2,1)S(1)}, u32[]{:S(2)}, u32[]{:S(2)}) collective-permute-start(bf16[128,4096]{1,0:T(8,128)(2,1)S(1)} %fold_near.1.w0), channel_id=1, source_target_pairs={{0,2},{1,7},{2,4},{3,1},{4,6},{5,3},{6,0},{7,5},{8,10},{9,15},{10,... | collective-permute-start | bytes 3145736 | tf_op jit(solution)/shard_map/ppermute | solution.py:386
  29.0 0.0 copy-start.3
  29.0 2.5 %fold_far.1.w0y = bf16[128,4096]{1,0:T(8,128)(2,1)S(1)} custom-call(bf16[1024,4096]{1,0:T(8,128)(2,1)} %weight_hbm.1), custom_call_target="tpu_custom_call" | custom-call | flops 4194304 | bytes 5242880 | tf_op jit(solution)/shard_map/fold_far/pallas_call | solution.py:162
  31.5 0.0 copy-start
  31.6 0.1 collective-permute-start.6
  31.7 0.0 copy-done.3
  31.7 2.6 %collective-permute-start.2 = (bf16[2048,256]{1,0:T(8,128)(2,1)S(1)}, bf16[2048,256]{1,0:T(8,128)(2,1)S(1)}, u32[]{:S(2)}, u32[]{:S(2)}) collective-permute-start(bf16[2048,256]{1,0:T(8,128)(2,1)S(1)} %copy-done.3), channel_id=1, source_target_pairs={{0,8},{1,25},{2,10},{3,27},{4,12},{5,29},{6,14},{7,31},{8,16},{9,1... | collective-permute-start | bytes 3145736 | tf_op jit(solution)/shard_map/ppermute | solution.py:387
  34.2 14.7 %collective-permute-done.7.w2 = bf16[128,4096]{1,0:T(8,128)(2,1)S(1)} collective-permute-done((bf16[128,4096]{1,0:T(8,128)(2,1)S(1)}, bf16[128,4096]{1,0:T(8,128)(2,1)S(1)}, u32[]{:S(2)}, u32[]{:S(2)}) %collective-permute-start.7) | collective-permute-done | bytes 1048608 | tf_op jit(solution)/shard_map/ppermute | solution.py:386
  49.0 3.3 %collective-permute-start.8 = (bf16[128,4096]{1,0:T(8,128)(2,1)S(1)}, bf16[128,4096]{1,0:T(8,128)(2,1)S(1)}, u32[]{:S(2)}, u32[]{:S(2)}) collective-permute-start(bf16[128,4096]{1,0:T(8,128)(2,1)S(1)} %collective-permute-done.7.w2), channel_id=1, source_target_pairs={{0,8},{1,25},{2,10},{3,27},{4,12},{5,29},{6,14},{7,31},{8,16},{9,1... | collective-permute-start | bytes 3145736 | tf_op jit(solution)/shard_map/ppermute | solution.py:387
  52.3 0.0 copy-done.1
  52.3 1.1 collective-permute-start.5
  53.4 0.0 collective-permute-done.v1
  53.4 0.1 collective-permute-start.3
  53.5 0.0 collective-permute-done.6.w1y
  53.5 0.4 collective-permute-start.9
  53.9 1.1 collective-permute-done.2.v2y
  55.0 2.9 %collective-permute-start.4 = (bf16[2048,256]{1,0:T(8,128)(2,1)S(1)}, bf16[2048,256]{1,0:T(8,128)(2,1)S(1)}, u32[]{:S(2)}, u32[]{:S(2)}) collective-permute-start(bf16[2048,256]{1,0:T(8,128)(2,1)S(1)} %collective-permute-done.2.v2y), channel_id=1, source_target_pairs={{0,1},{1,0},{2,3},{3,2},{4,5},{5,4},{6,7},{7,6},{8,9},{9,8},{10,11... | collective-permute-start | bytes 3145736 | tf_op jit(solution)/shard_map/ppermute | solution.py:388
  57.9 16.5 %collective-permute-done.8.w2y = bf16[128,4096]{1,0:T(8,128)(2,1)S(1)} collective-permute-done((bf16[128,4096]{1,0:T(8,128)(2,1)S(1)}, bf16[128,4096]{1,0:T(8,128)(2,1)S(1)}, u32[]{:S(2)}, u32[]{:S(2)}) %collective-permute-start.8) | collective-permute-done | bytes 1048608 | tf_op jit(solution)/shard_map/ppermute | solution.py:387
  74.4 3.2 %collective-permute-start.10 = (bf16[128,4096]{1,0:T(8,128)(2,1)S(1)}, bf16[128,4096]{1,0:T(8,128)(2,1)}, u32[]{:S(2)}, u32[]{:S(2)}) collective-permute-start(bf16[128,4096]{1,0:T(8,128)(2,1)S(1)} %collective-permute-done.8.w2y), channel_id=1, source_target_pairs={{0,1},{1,0},{2,3},{3,2},{4,5},{5,4},{6,7},{7,6},{8,9},{9,8},{10,11... | collective-permute-start | bytes 3145736 | tf_op jit(solution)/shard_map/ppermute | solution.py:388
  77.7 0.0 collective-permute-done.5.w1
  77.7 0.0 collective-permute-done.3.v3
  77.7 0.0 copy-done.4
  77.7 0.0 copy-start.9
  77.7 0.0 collective-permute-done.9.w3
  77.7 0.0 copy-done.5
  77.7 0.0 copy-start.10
  77.7 0.0 collective-permute-done.4.v3y
  77.7 0.0 copy-done.6
  77.7 0.0 copy-done.7
  77.7 0.9 copy-done.8
  78.6 0.4 copy-done.9
  79.0 0.3 copy-done.10
  79.3 1.0 copy-done.11
  80.3 0.0 collective-permute-done.10.w3y
  80.3 0.0 all-to-all-done
  80.3 0.0 copy-done
  80.3 11.6 %owner_best.1 = f32[256,128]{1,0:T(8,128)} custom-call(bf16[32,128]{1,0:T(8,128)(2,1)} %bitcast.14, bf16[8704,128]{1,0:T(8,128)(2,1)} %bitcast.4.got_hbm, bf16[4096,256]{1,0:T(8,128)(2,1)} %v0.1, bf16[4096,256]{1,0:T(8,128)(2,1)} %collective-permute-done.v1, bf16[2048,256]{1,0:T(8,128)(2,1)} %copy-done.2, bf16[2048,256]{1,0:T(8,128)(2,1)} %copy-done.6, ...), custom_call_target="tpu_custom_call" | custom-call | flops 6442450944 | bytes 20971520 | tf_op jit(solution)/shard_map/owner_best/pallas_call | solution.py:310
  91.8 22.3 %all_to_all.16 = f32[256,1,128]{2,1,0:T(1,128)} all-to-all(f32[256,1,128]{2,1,0:T(1,128)} %bitcast.11), channel_id=1, replica_groups=mesh['dp'=64,'tensor'=4] {'dp','tensor'}, dimensions={0} | all-to-all | bytes 262144 | tf_op jit(solution)/shard_map/all_to_all | solution.py:417
  114.1 1.9 %pick.1 = f32[1,512]{1,0:T(1,128)} custom-call(s32[8,512]{1,0:T(8,128)} %get-tuple-element.11.flat_ref, f32[256,128]{1,0:T(8,128)} %bitcast.10), custom_call_target="tpu_custom_call" | custom-call | tf_op jit(solution)/shard_map/pick/pallas_call | solution.py:351
  (6 shorter events, 0.0 us)
Async XLA Ops:
  5.6 17.9 %collective-permute-start.1 = (bf16[2048,256]{1,0:T(8,128)(2,1)}, bf16[2048,256]{1,0:T(8,128)(2,1)S(1)}, u32[]{:S(2)}, u32[]{:S(2)}) collective-permute-start(bf16[2048,256]{1,0:T(8,128)(2,1)} %get-tuple-element.13), channel_id=1, source_target_pairs={{0,2},{1,7},{2,4},{3,1},{4,6},{5,3},{6,0},{7,5},{8,10},{9,15},{10,... | collective-permute-start | bytes 3145736 | tf_op jit(solution)/shard_map/ppermute | solution.py:386
  9.0 44.4 %collective-permute-start = (bf16[4096,256]{1,0:T(8,128)(2,1)}, bf16[4096,256]{1,0:T(8,128)(2,1)}, u32[]{:S(2)}, u32[]{:S(2)}) collective-permute-start(bf16[4096,256]{1,0:T(8,128)(2,1)} %v0.1), channel_id=1, source_target_pairs={{0,1},{1,0},{2,3},{3,2},{4,5},{5,4},{6,7},{7,6},{8,9},{9,8},{10,11... | collective-permute-start | bytes 6291464 | tf_op jit(solution)/shard_map/ppermute | solution.py:407
  9.0 71.3 %all-to-all-start = ((bf16[256,17,2,128]{3,2,1,0:T(2,128)(2,1)}), bf16[256,17,2,128]{3,2,1,0:T(2,128)(2,1)}, u32[]{:S(2)}, u32[]{:S(2)}) async-start(bf16[256,17,2,128]{3,2,1,0:T(2,128)(2,1)} %bitcast.3), calls=%async_computation | async-start | bytes 4456448 | tf_op jit(solution)/shard_map/all_to_all | solution.py:408
  23.5 2.8 %copy-start.2 = (bf16[2048,256]{1,0:T(8,128)(2,1)}, bf16[2048,256]{1,0:T(8,128)(2,1)S(1)}, u32[]{:S(2)}) copy-start(bf16[2048,256]{1,0:T(8,128)(2,1)S(1)} %collective-permute-done.1.v2) | copy-start | bytes 3145732
  26.4 25.9 %copy-start.1 = (bf16[128,4096]{1,0:T(8,128)(2,1)}, bf16[128,4096]{1,0:T(8,128)(2,1)S(1)}, u32[]{:S(2)}) copy-start(bf16[128,4096]{1,0:T(8,128)(2,1)S(1)} %fold_near.1.w0) | copy-start | bytes 3145732
  26.4 22.6 %collective-permute-start.7 = (bf16[128,4096]{1,0:T(8,128)(2,1)S(1)}, bf16[128,4096]{1,0:T(8,128)(2,1)S(1)}, u32[]{:S(2)}, u32[]{:S(2)}) collective-permute-start(bf16[128,4096]{1,0:T(8,128)(2,1)S(1)} %fold_near.1.w0), channel_id=1, source_target_pairs={{0,2},{1,7},{2,4},{3,1},{4,6},{5,3},{6,0},{7,5},{8,10},{9,15},{10,... | collective-permute-start | bytes 3145736 | tf_op jit(solution)/shard_map/ppermute | solution.py:386
  29.0 2.6 %copy-start.3 = (bf16[2048,256]{1,0:T(8,128)(2,1)S(1)}, bf16[2048,256]{1,0:T(8,128)(2,1)}, u32[]{:S(2)}) copy-start(bf16[2048,256]{1,0:T(8,128)(2,1)} %copy-done.2) | copy-start | bytes 3145732
  31.5 48.7 %copy-start = (bf16[128,4096]{1,0:T(8,128)(2,1)}, bf16[128,4096]{1,0:T(8,128)(2,1)S(1)}, u32[]{:S(2)}) copy-start(bf16[128,4096]{1,0:T(8,128)(2,1)S(1)} %fold_far.1.w0y) | copy-start | bytes 3145732
  31.6 22.0 %collective-permute-start.6 = (bf16[128,4096]{1,0:T(8,128)(2,1)S(1)}, bf16[128,4096]{1,0:T(8,128)(2,1)S(1)}, u32[]{:S(2)}, u32[]{:S(2)}) collective-permute-start(bf16[128,4096]{1,0:T(8,128)(2,1)S(1)} %fold_far.1.w0y), channel_id=1, source_target_pairs={{0,1},{1,0},{2,3},{3,2},{4,5},{5,4},{6,7},{7,6},{8,9},{9,8},{10,11... | collective-permute-start | bytes 3145736 | tf_op jit(solution)/shard_map/ppermute | solution.py:414
  31.7 23.3 %collective-permute-start.2 = (bf16[2048,256]{1,0:T(8,128)(2,1)S(1)}, bf16[2048,256]{1,0:T(8,128)(2,1)S(1)}, u32[]{:S(2)}, u32[]{:S(2)}) collective-permute-start(bf16[2048,256]{1,0:T(8,128)(2,1)S(1)} %copy-done.3), channel_id=1, source_target_pairs={{0,8},{1,25},{2,10},{3,27},{4,12},{5,29},{6,14},{7,31},{8,16},{9,1... | collective-permute-start | bytes 3145736 | tf_op jit(solution)/shard_map/ppermute | solution.py:387
  49.0 28.7 %copy-start.4 = (bf16[128,4096]{1,0:T(8,128)(2,1)}, bf16[128,4096]{1,0:T(8,128)(2,1)S(1)}, u32[]{:S(2)}) copy-start(bf16[128,4096]{1,0:T(8,128)(2,1)S(1)} %collective-permute-done.7.w2) | copy-start | bytes 3145732
  49.0 25.5 %collective-permute-start.8 = (bf16[128,4096]{1,0:T(8,128)(2,1)S(1)}, bf16[128,4096]{1,0:T(8,128)(2,1)S(1)}, u32[]{:S(2)}, u32[]{:S(2)}) collective-permute-start(bf16[128,4096]{1,0:T(8,128)(2,1)S(1)} %collective-permute-done.7.w2), channel_id=1, source_target_pairs={{0,8},{1,25},{2,10},{3,27},{4,12},{5,29},{6,14},{7,31},{8,16},{9,1... | collective-permute-start | bytes 3145736 | tf_op jit(solution)/shard_map/ppermute | solution.py:387
  52.3 25.4 %collective-permute-start.5 = (bf16[128,4096]{1,0:T(8,128)(2,1)S(1)}, bf16[128,4096]{1,0:T(8,128)(2,1)S(1)}, u32[]{:S(2)}, u32[]{:S(2)}) collective-permute-start(bf16[128,4096]{1,0:T(8,128)(2,1)S(1)} %fold_near.1.w0), channel_id=1, source_target_pairs={{0,1},{1,0},{2,3},{3,2},{4,5},{5,4},{6,7},{7,6},{8,9},{9,8},{10,11... | collective-permute-start | bytes 3145736 | tf_op jit(solution)/shard_map/ppermute | solution.py:414
  53.4 24.3 %collective-permute-start.3 = (bf16[2048,256]{1,0:T(8,128)(2,1)S(1)}, bf16[2048,256]{1,0:T(8,128)(2,1)S(1)}, u32[]{:S(2)}, u32[]{:S(2)}) collective-permute-start(bf16[2048,256]{1,0:T(8,128)(2,1)S(1)} %copy-done.3), channel_id=1, source_target_pairs={{0,1},{1,0},{2,3},{3,2},{4,5},{5,4},{6,7},{7,6},{8,9},{9,8},{10,11... | collective-permute-start | bytes 3145736 | tf_op jit(solution)/shard_map/ppermute | solution.py:388
  53.5 24.2 %copy-start.5 = (bf16[128,4096]{1,0:T(8,128)(2,1)}, bf16[128,4096]{1,0:T(8,128)(2,1)S(1)}, u32[]{:S(2)}) copy-start(bf16[128,4096]{1,0:T(8,128)(2,1)S(1)} %collective-permute-done.6.w1y) | copy-start | bytes 3145732
  53.5 24.2 %collective-permute-start.9 = (bf16[128,4096]{1,0:T(8,128)(2,1)S(1)}, bf16[128,4096]{1,0:T(8,128)(2,1)S(1)}, u32[]{:S(2)}, u32[]{:S(2)}) collective-permute-start(bf16[128,4096]{1,0:T(8,128)(2,1)S(1)} %collective-permute-done.7.w2), channel_id=1, source_target_pairs={{0,1},{1,0},{2,3},{3,2},{4,5},{5,4},{6,7},{7,6},{8,9},{9,8},{10,11... | collective-permute-start | bytes 3145736 | tf_op jit(solution)/shard_map/ppermute | solution.py:388
  55.0 22.7 %copy-start.6 = (bf16[2048,256]{1,0:T(8,128)(2,1)}, bf16[2048,256]{1,0:T(8,128)(2,1)S(1)}, u32[]{:S(2)}) copy-start(bf16[2048,256]{1,0:T(8,128)(2,1)S(1)} %collective-permute-done.2.v2y) | copy-start | bytes 3145732
  55.0 22.7 %collective-permute-start.4 = (bf16[2048,256]{1,0:T(8,128)(2,1)S(1)}, bf16[2048,256]{1,0:T(8,128)(2,1)S(1)}, u32[]{:S(2)}, u32[]{:S(2)}) collective-permute-start(bf16[2048,256]{1,0:T(8,128)(2,1)S(1)} %collective-permute-done.2.v2y), channel_id=1, source_target_pairs={{0,1},{1,0},{2,3},{3,2},{4,5},{5,4},{6,7},{7,6},{8,9},{9,8},{10,11... | collective-permute-start | bytes 3145736 | tf_op jit(solution)/shard_map/ppermute | solution.py:388
  74.4 3.3 %copy-start.7 = (bf16[128,4096]{1,0:T(8,128)(2,1)}, bf16[128,4096]{1,0:T(8,128)(2,1)S(1)}, u32[]{:S(2)}) copy-start(bf16[128,4096]{1,0:T(8,128)(2,1)S(1)} %collective-permute-done.8.w2y) | copy-start | bytes 3145732
  74.4 5.8 %collective-permute-start.10 = (bf16[128,4096]{1,0:T(8,128)(2,1)S(1)}, bf16[128,4096]{1,0:T(8,128)(2,1)}, u32[]{:S(2)}, u32[]{:S(2)}) collective-permute-start(bf16[128,4096]{1,0:T(8,128)(2,1)S(1)} %collective-permute-done.8.w2y), channel_id=1, source_target_pairs={{0,1},{1,0},{2,3},{3,2},{4,5},{5,4},{6,7},{7,6},{8,9},{9,8},{10,11... | collective-permute-start | bytes 3145736 | tf_op jit(solution)/shard_map/ppermute | solution.py:388
  77.7 1.0 copy-start.8
  77.7 1.3 %copy-start.9 = (bf16[2048,256]{1,0:T(8,128)(2,1)}, bf16[2048,256]{1,0:T(8,128)(2,1)S(1)}, u32[]{:S(2)}) copy-start(bf16[2048,256]{1,0:T(8,128)(2,1)S(1)} %collective-permute-done.3.v3) | copy-start | bytes 3145732
  77.7 1.6 %copy-start.10 = (bf16[128,4096]{1,0:T(8,128)(2,1)}, bf16[128,4096]{1,0:T(8,128)(2,1)S(1)}, u32[]{:S(2)}) copy-start(bf16[128,4096]{1,0:T(8,128)(2,1)S(1)} %collective-permute-done.9.w3) | copy-start | bytes 3145732
  79.3 1.0 copy-start.11

commit v5 on v4

--- a/solution.py
+++ b/solution.py
@@ -381,13 +381,6 @@
     return pairs
 
 
-def cross(near, splits, owners):
-    swap = [(t, t ^ 1) for t in range(splits)]
-    across = lax.ppermute(near, AXES, ring_pairs(splits, owners))
-    along = lax.ppermute(across, AXES, column_pairs(splits, owners))
-    return [across, along, lax.ppermute(across, "tensor", swap), lax.ppermute(along, "tensor", swap)]
-
-
 def shards(final_input, norm_gain, value_weight, out_weight, cluster, priority):
     rows, width = final_input.shape
     splits = lax.axis_size("tensor")
@@ -404,15 +397,20 @@
         owners * rows,
     )
     swap = [(t, t ^ 1) for t in range(splits)]
-    projects = [value_weight, lax.ppermute(value_weight, "tensor", swap), *cross(half, splits, owners)]
+    v_across = lax.ppermute(half, AXES, ring_pairs(splits, owners))
+    v_along = lax.ppermute(v_across, AXES, column_pairs(splits, owners))
     got = lax.all_to_all(message.reshape(clusters, depth // 2, 2, LANES), AXES, 0, 0, tiled=True)
     got = got.reshape(clusters * depth, LANES)
-    out_weight, _, _ = lax.optimization_barrier((out_weight, flat, projects[2]))
+    out_weight, _, _ = lax.optimization_barrier((out_weight, flat, v_across))
     near = fold(out_weight, True)
     out_weight, near = lax.optimization_barrier((out_weight, near))
     far = fold(out_weight, False)
     beside = [lax.ppermute(w, "tensor", swap) for w in (near, far)]
-    weights = [near, far, *beside, *cross(near, splits, owners)]
+    across = [lax.ppermute(w, AXES, ring_pairs(splits, owners)) for w in (near, far)]
+    across[1], v_along = lax.optimization_barrier((across[1], v_along))
+    weights = [near, far, *beside, *across, *[lax.ppermute(w, "tensor", swap) for w in across]]
+    projects = [value_weight, lax.ppermute(value_weight, "tensor", swap), v_across, v_along]
+    projects += [lax.ppermute(w, "tensor", swap) for w in (v_across, v_along)]
     best = owner_best(norm_gain.reshape(blocks(width), LANES), got, projects, weights, clusters)
     returned = lax.all_to_all(best, AXES, 0, 0, tiled=True)
     return pick(flat, returned).reshape(rows)

time: 116 us -> 117 us (level)
  waiting for transfers between devices: 32.4 us -> 33.8 us
  starting transfers between devices: 34.3 us -> 33 us
    ppermute x8, starting transfers between devices: 18.6 us -> 14.7 us  [the longest x2 4.17 us: shards(): lax.ppermute(w, 'tensor', swap)]
    ppermute x2, starting transfers between devices: 1.21 us -> 3.78 us  [shards(): beside = [lax.ppermute(w, 'tensor', swap) for w in (near, far)]]
    ppermute x8, waiting for transfers between devices: 32.3 us -> 33.8 us  [the longest x2 31.8 us: shards(): lax.ppermute(w, AXES, ring_pairs(splits, owners))]
  transfers between devices with their start and end apart: 12 -> 12, of which waited for: 3 -> 3; matrix products, arithmetic and copies ran while one was open for 0% -> 0% of each run, Pallas kernels for 5% -> 4%
where the time goes in v5:
time: 117 us
  waiting for transfers between devices  33.8 us (29%)
  starting transfers between devices  33 us (28%)
  Pallas kernels  24.2 us (21%)
  blocking collectives  22.8 us (19%)
  local copies, waits for them, and re-layouts  2.93 us (3%)
    ppermute x2, waiting for transfers between devices, shards(): lax.ppermute(w, AXES, ring_pairs(splits, owners))  31.8 us
    all_to_all x1, blocking collectives, shards(): returned = lax.all_to_all(best, AXES, 0, 0, tiled=True)  22.8 us
    all_to_all x1, starting transfers between devices, shards(): lax.all_to_all(message.reshape(clusters, depth // 2, 2, LANES), AXES, 0,...  14.5 us
    pallas_call x1, Pallas kernels, owner_best(): pl.pallas_call(owner_kernel, in_specs=[vmem] + [hbm] * (1 + len(projects)...  11.6 us
    pallas_call x1, Pallas kernels, pack(): pl.pallas_call(functools.partial(pack_kernel, sentinel), in_specs=[vmem,...  5.58 us
    pallas_call x2, Pallas kernels, fold(): pl.pallas_call(functools.partial(fold_kernel, near), in_specs=[hbm], out_...  5.23 us
    ppermute x2, starting transfers between devices, shards(): lax.ppermute(w, 'tensor', swap)  4.17 us
    ppermute x2, starting transfers between devices, shards(): beside = [lax.ppermute(w, 'tensor', swap) for w in (near, far)]  3.78 us
  transfers between devices with their start and end apart: 12, of which 3 were waited for; matrix products, arithmetic and copies ran while one was open for 0% of the time, Pallas kernels for 4%

profile of v5, /device:TPU:1, one launch (start us, length us, event | category | flops | bytes accessed | tf_op | source)
XLA Modules:
  0.0 116.9 jit_solution(14576174121629532743)
XLA Ops:
  0.0 5.6 %pack.1 = (s32[8,512]{1,0:T(8,128)}, bf16[8704,128]{1,0:T(8,128)(2,1)}, bf16[2048,256]{1,0:T(8,128)(2,1)}) custom-call(s32[1,512]{1,0:T(1,128)} %bitcast.12, s32[1,512]{1,0:T(1,128)} %bitcast.13, bf16[512,4096]{1,0:T(8,128)(2,1)} %x_hbm.1, bf16[4096,256]{1,0:T(8,128)(2,1)} %v0.1), custom_call_target="tpu_custom_call" | custom-call | flops 1073741824 | bytes 6291456 | tf_op jit(solution)/shard_map/pack/pallas_call | solution.py:106
  5.6 3.4 %collective-permute-start.1 = (bf16[2048,256]{1,0:T(8,128)(2,1)}, bf16[2048,256]{1,0:T(8,128)(2,1)S(1)}, u32[]{:S(2)}, u32[]{:S(2)}) collective-permute-start(bf16[2048,256]{1,0:T(8,128)(2,1)} %get-tuple-element.15), channel_id=1, source_target_pairs={{0,2},{1,7},{2,4},{3,1},{4,6},{5,3},{6,0},{7,5},{8,10},{9,15},{10,... | collective-permute-start | bytes 3145736 | tf_op jit(solution)/shard_map/ppermute | solution.py:400
  9.0 0.0 collective-permute-start
  9.0 14.5 %all-to-all-start = ((bf16[256,17,2,128]{3,2,1,0:T(2,128)(2,1)}), bf16[256,17,2,128]{3,2,1,0:T(2,128)(2,1)}, u32[]{:S(2)}, u32[]{:S(2)}) async-start(bf16[256,17,2,128]{3,2,1,0:T(2,128)(2,1)} %bitcast.3), calls=%async_computation | async-start | bytes 4456448 | tf_op jit(solution)/shard_map/all_to_all | solution.py:402
  23.5 0.0 collective-permute-done.1.v2
  23.5 0.0 copy-start.2
  23.5 1.0 copy-done.2
  24.5 2.4 %fold_near.1.w0 = bf16[128,4096]{1,0:T(8,128)(2,1)S(1)} custom-call(bf16[1024,4096]{1,0:T(8,128)(2,1)} %weight_hbm.1), custom_call_target="tpu_custom_call" | custom-call | flops 399999991808 | bytes 5242880 | tf_op jit(solution)/shard_map/fold_near/pallas_call | solution.py:162
  26.9 0.0 copy-start.1
  26.9 0.0 copy-start.3
  26.9 2.8 %fold_far.1.w0y = bf16[128,4096]{1,0:T(8,128)(2,1)S(1)} custom-call(bf16[1024,4096]{1,0:T(8,128)(2,1)} %weight_hbm.1), custom_call_target="tpu_custom_call" | custom-call | flops 4194304 | bytes 5242880 | tf_op jit(solution)/shard_map/fold_far/pallas_call | solution.py:162
  29.8 0.0 copy-start
  29.8 2.7 %collective-permute-start.2 = (bf16[128,4096]{1,0:T(8,128)(2,1)S(1)}, bf16[128,4096]{1,0:T(8,128)(2,1)S(1)}, u32[]{:S(2)}, u32[]{:S(2)}) collective-permute-start(bf16[128,4096]{1,0:T(8,128)(2,1)S(1)} %fold_far.1.w0y), channel_id=1, source_target_pairs={{0,2},{1,7},{2,4},{3,1},{4,6},{5,3},{6,0},{7,5},{8,10},{9,15},{10,... | collective-permute-start | bytes 3145736 | tf_op jit(solution)/shard_map/ppermute | solution.py:409
  32.5 0.0 copy-done.3
  32.5 2.5 %collective-permute-start.3 = (bf16[2048,256]{1,0:T(8,128)(2,1)S(1)}, bf16[2048,256]{1,0:T(8,128)(2,1)S(1)}, u32[]{:S(2)}, u32[]{:S(2)}) collective-permute-start(bf16[2048,256]{1,0:T(8,128)(2,1)S(1)} %copy-done.3), channel_id=1, source_target_pairs={{0,8},{1,25},{2,10},{3,27},{4,12},{5,29},{6,14},{7,31},{8,16},{9,1... | collective-permute-start | bytes 3145736 | tf_op jit(solution)/shard_map/ppermute | solution.py:401
  35.0 0.6 collective-permute-start.8
  35.5 0.0 collective-permute-start.7
  35.5 17.3 %collective-permute-done.2.w2y = bf16[128,4096]{1,0:T(8,128)(2,1)S(1)} collective-permute-done((bf16[128,4096]{1,0:T(8,128)(2,1)S(1)}, bf16[128,4096]{1,0:T(8,128)(2,1)S(1)}, u32[]{:S(2)}, u32[]{:S(2)}) %collective-permute-start.2) | collective-permute-done | bytes 1048608 | tf_op jit(solution)/shard_map/ppermute | solution.py:409
  52.8 0.0 copy-done.1
  52.8 0.0 copy-start.4
  52.8 3.8 %collective-permute-start.6 = (bf16[128,4096]{1,0:T(8,128)(2,1)S(1)}, bf16[128,4096]{1,0:T(8,128)(2,1)S(1)}, u32[]{:S(2)}, u32[]{:S(2)}) collective-permute-start(bf16[128,4096]{1,0:T(8,128)(2,1)S(1)} %fold_near.1.w0), channel_id=1, source_target_pairs={{0,1},{1,0},{2,3},{3,2},{4,5},{5,4},{6,7},{7,6},{8,9},{9,8},{10,11... | collective-permute-start | bytes 3145736 | tf_op jit(solution)/shard_map/ppermute | solution.py:408
  56.6 0.0 collective-permute-done.3.v2y
  56.6 1.3 %collective-permute-start.4 = (bf16[2048,256]{1,0:T(8,128)(2,1)S(1)}, bf16[2048,256]{1,0:T(8,128)(2,1)S(1)}, u32[]{:S(2)}, u32[]{:S(2)}) collective-permute-start(bf16[2048,256]{1,0:T(8,128)(2,1)S(1)} %copy-done.3), channel_id=1, source_target_pairs={{0,1},{1,0},{2,3},{3,2},{4,5},{5,4},{6,7},{7,6},{8,9},{9,8},{10,11... | collective-permute-start | bytes 3145736 | tf_op jit(solution)/shard_map/ppermute | solution.py:413
  57.9 0.0 collective-permute-done.v1
  57.9 0.1 collective-permute-start.5
  58.0 14.5 %collective-permute-done.8.w2 = bf16[128,4096]{1,0:T(8,128)(2,1)S(1)} collective-permute-done((bf16[128,4096]{1,0:T(8,128)(2,1)S(1)}, bf16[128,4096]{1,0:T(8,128)(2,1)S(1)}, u32[]{:S(2)}, u32[]{:S(2)}) %collective-permute-start.8) | collective-permute-done | bytes 1048608 | tf_op jit(solution)/shard_map/ppermute | solution.py:409
  72.5 3.9 %collective-permute-start.9 = (bf16[128,4096]{1,0:T(8,128)(2,1)S(1)}, bf16[128,4096]{1,0:T(8,128)(2,1)S(1)}, u32[]{:S(2)}, u32[]{:S(2)}) collective-permute-start(bf16[128,4096]{1,0:T(8,128)(2,1)S(1)} %collective-permute-done.8.w2), channel_id=1, source_target_pairs={{0,1},{1,0},{2,3},{3,2},{4,5},{5,4},{6,7},{7,6},{8,9},{9,8},{10,11... | collective-permute-start | bytes 3145736 | tf_op jit(solution)/shard_map/ppermute | solution.py:411
  76.4 0.0 collective-permute-done.7.w1y
  76.4 0.3 collective-permute-start.10
  76.7 0.0 collective-permute-done.6.w1
  76.7 0.0 collective-permute-done.4.v3
  76.7 0.0 copy-done.4
  76.7 0.0 copy-start.9
  76.7 2.0 %collective-permute-done.9.w3 = bf16[128,4096]{1,0:T(8,128)(2,1)S(1)} collective-permute-done((bf16[128,4096]{1,0:T(8,128)(2,1)S(1)}, bf16[128,4096]{1,0:T(8,128)(2,1)S(1)}, u32[]{:S(2)}, u32[]{:S(2)}) %collective-permute-start.9) | collective-permute-done | bytes 1048608 | tf_op jit(solution)/shard_map/ppermute | solution.py:411
  78.7 0.0 copy-done.5
  78.7 0.0 collective-permute-done.5.v3y
  78.7 0.0 copy-done.6
  78.7 0.0 copy-done.7
  78.7 0.0 copy-done.8
  78.7 0.0 copy-done.9
  78.7 0.9 copy-done.11
  79.7 1.0 copy-done.10
  80.7 0.0 collective-permute-done.10.w3y
  80.7 0.0 all-to-all-done
  80.7 0.0 copy-done
  80.7 11.6 %owner_best.1 = f32[256,128]{1,0:T(8,128)} custom-call(bf16[32,128]{1,0:T(8,128)(2,1)} %bitcast.14, bf16[8704,128]{1,0:T(8,128)(2,1)} %bitcast.4.got_hbm, bf16[4096,256]{1,0:T(8,128)(2,1)} %v0.1, bf16[4096,256]{1,0:T(8,128)(2,1)} %collective-permute-done.v1, bf16[2048,256]{1,0:T(8,128)(2,1)} %copy-done.2, bf16[2048,256]{1,0:T(8,128)(2,1)} %copy-done.5, ...), custom_call_target="tpu_custom_call" | custom-call | flops 6442450944 | bytes 20971520 | tf_op jit(solution)/shard_map/owner_best/pallas_call | solution.py:310
  92.3 22.8 %all_to_all.16 = f32[256,1,128]{2,1,0:T(1,128)} all-to-all(f32[256,1,128]{2,1,0:T(1,128)} %bitcast.11), channel_id=1, replica_groups=mesh['dp'=64,'tensor'=4] {'dp','tensor'}, dimensions={0} | all-to-all | bytes 262144 | tf_op jit(solution)/shard_map/all_to_all | solution.py:415
  115.0 1.9 %pick.1 = f32[1,512]{1,0:T(1,128)} custom-call(s32[8,512]{1,0:T(8,128)} %get-tuple-element.13.flat_ref, f32[256,128]{1,0:T(8,128)} %bitcast.10), custom_call_target="tpu_custom_call" | custom-call | tf_op jit(solution)/shard_map/pick/pallas_call | solution.py:351
  (6 shorter events, 0.0 us)
Async XLA Ops:
  5.6 17.9 %collective-permute-start.1 = (bf16[2048,256]{1,0:T(8,128)(2,1)}, bf16[2048,256]{1,0:T(8,128)(2,1)S(1)}, u32[]{:S(2)}, u32[]{:S(2)}) collective-permute-start(bf16[2048,256]{1,0:T(8,128)(2,1)} %get-tuple-element.15), channel_id=1, source_target_pairs={{0,2},{1,7},{2,4},{3,1},{4,6},{5,3},{6,0},{7,5},{8,10},{9,15},{10,... | collective-permute-start | bytes 3145736 | tf_op jit(solution)/shard_map/ppermute | solution.py:400
  9.0 48.9 %collective-permute-start = (bf16[4096,256]{1,0:T(8,128)(2,1)}, bf16[4096,256]{1,0:T(8,128)(2,1)}, u32[]{:S(2)}, u32[]{:S(2)}) collective-permute-start(bf16[4096,256]{1,0:T(8,128)(2,1)} %v0.1), channel_id=1, source_target_pairs={{0,1},{1,0},{2,3},{3,2},{4,5},{5,4},{6,7},{7,6},{8,9},{9,8},{10,11... | collective-permute-start | bytes 6291464 | tf_op jit(solution)/shard_map/ppermute | solution.py:412
  9.0 71.7 %all-to-all-start = ((bf16[256,17,2,128]{3,2,1,0:T(2,128)(2,1)}), bf16[256,17,2,128]{3,2,1,0:T(2,128)(2,1)}, u32[]{:S(2)}, u32[]{:S(2)}) async-start(bf16[256,17,2,128]{3,2,1,0:T(2,128)(2,1)} %bitcast.3), calls=%async_computation | async-start | bytes 4456448 | tf_op jit(solution)/shard_map/all_to_all | solution.py:402
  23.5 1.0 copy-start.2
  26.9 25.9 %copy-start.1 = (bf16[128,4096]{1,0:T(8,128)(2,1)}, bf16[128,4096]{1,0:T(8,128)(2,1)S(1)}, u32[]{:S(2)}) copy-start(bf16[128,4096]{1,0:T(8,128)(2,1)S(1)} %fold_near.1.w0) | copy-start | bytes 3145732
  26.9 5.5 %copy-start.3 = (bf16[2048,256]{1,0:T(8,128)(2,1)S(1)}, bf16[2048,256]{1,0:T(8,128)(2,1)}, u32[]{:S(2)}) copy-start(bf16[2048,256]{1,0:T(8,128)(2,1)} %copy-done.2) | copy-start | bytes 3145732
  29.8 50.9 %copy-start = (bf16[128,4096]{1,0:T(8,128)(2,1)}, bf16[128,4096]{1,0:T(8,128)(2,1)S(1)}, u32[]{:S(2)}) copy-start(bf16[128,4096]{1,0:T(8,128)(2,1)S(1)} %fold_far.1.w0y) | copy-start | bytes 3145732
  29.8 23.0 %collective-permute-start.2 = (bf16[128,4096]{1,0:T(8,128)(2,1)S(1)}, bf16[128,4096]{1,0:T(8,128)(2,1)S(1)}, u32[]{:S(2)}, u32[]{:S(2)}) collective-permute-start(bf16[128,4096]{1,0:T(8,128)(2,1)S(1)} %fold_far.1.w0y), channel_id=1, source_target_pairs={{0,2},{1,7},{2,4},{3,1},{4,6},{5,3},{6,0},{7,5},{8,10},{9,15},{10,... | collective-permute-start | bytes 3145736 | tf_op jit(solution)/shard_map/ppermute | solution.py:409
  32.5 24.1 %collective-permute-start.3 = (bf16[2048,256]{1,0:T(8,128)(2,1)S(1)}, bf16[2048,256]{1,0:T(8,128)(2,1)S(1)}, u32[]{:S(2)}, u32[]{:S(2)}) collective-permute-start(bf16[2048,256]{1,0:T(8,128)(2,1)S(1)} %copy-done.3), channel_id=1, source_target_pairs={{0,8},{1,25},{2,10},{3,27},{4,12},{5,29},{6,14},{7,31},{8,16},{9,1... | collective-permute-start | bytes 3145736 | tf_op jit(solution)/shard_map/ppermute | solution.py:401
  35.0 37.6 %collective-permute-start.8 = (bf16[128,4096]{1,0:T(8,128)(2,1)S(1)}, bf16[128,4096]{1,0:T(8,128)(2,1)S(1)}, u32[]{:S(2)}, u32[]{:S(2)}) collective-permute-start(bf16[128,4096]{1,0:T(8,128)(2,1)S(1)} %fold_near.1.w0), channel_id=1, source_target_pairs={{0,2},{1,7},{2,4},{3,1},{4,6},{5,3},{6,0},{7,5},{8,10},{9,15},{10,... | collective-permute-start | bytes 3145736 | tf_op jit(solution)/shard_map/ppermute | solution.py:409
  35.5 40.9 %collective-permute-start.7 = (bf16[128,4096]{1,0:T(8,128)(2,1)S(1)}, bf16[128,4096]{1,0:T(8,128)(2,1)S(1)}, u32[]{:S(2)}, u32[]{:S(2)}) collective-permute-start(bf16[128,4096]{1,0:T(8,128)(2,1)S(1)} %fold_far.1.w0y), channel_id=1, source_target_pairs={{0,1},{1,0},{2,3},{3,2},{4,5},{5,4},{6,7},{7,6},{8,9},{9,8},{10,11... | collective-permute-start | bytes 3145736 | tf_op jit(solution)/shard_map/ppermute | solution.py:408
  52.8 23.9 %copy-start.4 = (bf16[128,4096]{1,0:T(8,128)(2,1)}, bf16[128,4096]{1,0:T(8,128)(2,1)S(1)}, u32[]{:S(2)}) copy-start(bf16[128,4096]{1,0:T(8,128)(2,1)S(1)} %collective-permute-done.2.w2y) | copy-start | bytes 3145732
  52.8 23.9 %collective-permute-start.6 = (bf16[128,4096]{1,0:T(8,128)(2,1)S(1)}, bf16[128,4096]{1,0:T(8,128)(2,1)S(1)}, u32[]{:S(2)}, u32[]{:S(2)}) collective-permute-start(bf16[128,4096]{1,0:T(8,128)(2,1)S(1)} %fold_near.1.w0), channel_id=1, source_target_pairs={{0,1},{1,0},{2,3},{3,2},{4,5},{5,4},{6,7},{7,6},{8,9},{9,8},{10,11... | collective-permute-start | bytes 3145736 | tf_op jit(solution)/shard_map/ppermute | solution.py:408
  56.6 22.1 %copy-start.5 = (bf16[2048,256]{1,0:T(8,128)(2,1)}, bf16[2048,256]{1,0:T(8,128)(2,1)S(1)}, u32[]{:S(2)}) copy-start(bf16[2048,256]{1,0:T(8,128)(2,1)S(1)} %collective-permute-done.3.v2y) | copy-start | bytes 3145732
  56.6 20.1 %collective-permute-start.4 = (bf16[2048,256]{1,0:T(8,128)(2,1)S(1)}, bf16[2048,256]{1,0:T(8,128)(2,1)S(1)}, u32[]{:S(2)}, u32[]{:S(2)}) collective-permute-start(bf16[2048,256]{1,0:T(8,128)(2,1)S(1)} %copy-done.3), channel_id=1, source_target_pairs={{0,1},{1,0},{2,3},{3,2},{4,5},{5,4},{6,7},{7,6},{8,9},{9,8},{10,11... | collective-permute-start | bytes 3145736 | tf_op jit(solution)/shard_map/ppermute | solution.py:413
  57.9 20.8 %collective-permute-start.5 = (bf16[2048,256]{1,0:T(8,128)(2,1)S(1)}, bf16[2048,256]{1,0:T(8,128)(2,1)S(1)}, u32[]{:S(2)}, u32[]{:S(2)}) collective-permute-start(bf16[2048,256]{1,0:T(8,128)(2,1)S(1)} %collective-permute-done.3.v2y), channel_id=1, source_target_pairs={{0,1},{1,0},{2,3},{3,2},{4,5},{5,4},{6,7},{7,6},{8,9},{9,8},{10,11... | collective-permute-start | bytes 3145736 | tf_op jit(solution)/shard_map/ppermute | solution.py:413
  72.5 6.2 %copy-start.6 = (bf16[128,4096]{1,0:T(8,128)(2,1)}, bf16[128,4096]{1,0:T(8,128)(2,1)S(1)}, u32[]{:S(2)}) copy-start(bf16[128,4096]{1,0:T(8,128)(2,1)S(1)} %collective-permute-done.8.w2) | copy-start | bytes 3145732
  72.5 6.2 %collective-permute-start.9 = (bf16[128,4096]{1,0:T(8,128)(2,1)S(1)}, bf16[128,4096]{1,0:T(8,128)(2,1)S(1)}, u32[]{:S(2)}, u32[]{:S(2)}) collective-permute-start(bf16[128,4096]{1,0:T(8,128)(2,1)S(1)} %collective-permute-done.8.w2), channel_id=1, source_target_pairs={{0,1},{1,0},{2,3},{3,2},{4,5},{5,4},{6,7},{7,6},{8,9},{9,8},{10,11... | collective-permute-start | bytes 3145736 | tf_op jit(solution)/shard_map/ppermute | solution.py:411
  76.4 2.3 %copy-start.7 = (bf16[128,4096]{1,0:T(8,128)(2,1)}, bf16[128,4096]{1,0:T(8,128)(2,1)S(1)}, u32[]{:S(2)}) copy-start(bf16[128,4096]{1,0:T(8,128)(2,1)S(1)} %collective-permute-done.7.w1y) | copy-start | bytes 3145732
  76.4 4.3 %collective-permute-start.10 = (bf16[128,4096]{1,0:T(8,128)(2,1)S(1)}, bf16[128,4096]{1,0:T(8,128)(2,1)}, u32[]{:S(2)}, u32[]{:S(2)}) collective-permute-start(bf16[128,4096]{1,0:T(8,128)(2,1)S(1)} %collective-permute-done.2.w2y), channel_id=1, source_target_pairs={{0,1},{1,0},{2,3},{3,2},{4,5},{5,4},{6,7},{7,6},{8,9},{9,8},{10,11... | collective-permute-start | bytes 3145736 | tf_op jit(solution)/shard_map/ppermute | solution.py:411
  76.7 2.0 %copy-start.8 = (bf16[128,4096]{1,0:T(8,128)(2,1)}, bf16[128,4096]{1,0:T(8,128)(2,1)S(1)}, u32[]{:S(2)}) copy-start(bf16[128,4096]{1,0:T(8,128)(2,1)S(1)} %collective-permute-done.6.w1) | copy-start | bytes 3145732
  76.7 2.0 %copy-start.9 = (bf16[2048,256]{1,0:T(8,128)(2,1)}, bf16[2048,256]{1,0:T(8,128)(2,1)S(1)}, u32[]{:S(2)}) copy-start(bf16[2048,256]{1,0:T(8,128)(2,1)S(1)} %collective-permute-done.4.v3) | copy-start | bytes 3145732
  78.7 1.0 copy-start.11
  79.7 1.0 copy-start.10
